TPU v7x, 32 devices: a whole 2x2x4 slice. The times are simulated.
32 devices in a mesh: dp: 16 (over z, y, x), section: 2 (over core).
Axes of the slice: x: 2, y: 2, z: 4, core: 2. Of those that a mesh axis runs over, the one named last changes fastest.
Arguments:
- token_ids: int32 [2, 16, 512], P(None, 'dp'), may hold values from 0 to 119551
- lengths: int32 [2, 16], P(None, 'dp'), may hold values from 128 to 512, as said below
- positions: int32 [2, 16, 32], P(None, 'dp'), may hold values from 0 to 511, as said below
- targets: int32 [2, 16, 32], P(None, 'dp'), may hold values from 0 to 119551
- loss_weights: int32 [2, 16, 32], P(None, 'dp'), may hold values from 1 to 5
- embed_table: bfloat16 [119552, 768], P('dp')
- pos_table: bfloat16 [512, 768], replicated, may hold values from -3 to 3
- norm_params: float32 [2, 6, 768], P('section')
- base_qkv: bfloat16 [2, 768, 2304], P('section'), may hold values from -0.21875 to 0.21875
- base_out: bfloat16 [2, 768, 768], P('section'), may hold values from -2.5 to 2.5
- base_up: bfloat16 [2, 768, 3072], P('section'), may hold values from -0.21875 to 0.21875
- base_down: bfloat16 [2, 3072, 768], P('section'), may hold values from -0.109375 to 0.109375
- master: float32 [2, 320, 48, 48], P('section', 'dp'), may hold values from -0.3125 to 0.3125
- momentum: float32 [2, 320, 48, 48], P('section', 'dp'), may hold values from -0.00024414062 to 0.00024414062
- stat_left: float32 [2, 320, 48, 48], P('section', 'dp')
- stat_right: float32 [2, 320, 48, 48], P('section', 'dp')
- root_left: float32 [2, 320, 48, 48], P('section', 'dp')
- root_right: float32 [2, 320, 48, 48], P('section', 'dp')
- vectors: float32 [2, 1728], P('section', 'dp'), may hold values from -3 to 3
- vec_first: float32 [2, 1728], P('section', 'dp'), may hold values from -7.6293945e-05 to 7.6293945e-05
- vec_second: float32 [2, 1728], P('section', 'dp'), may hold values from 2.4414062e-12 to 9.765625e-12
Outputs:
- grad_blocks: float32 [2, 320, 48, 48], P('section', 'dp')
- momentum_new: float32 [2, 320, 48, 48], P('section', 'dp')
- left_new: float32 [2, 320, 48, 48], P('section', 'dp')
- right_new: float32 [2, 320, 48, 48], P('section', 'dp')
- master_new: float32 [2, 320, 48, 48], P('section', 'dp')
- master_low: bfloat16 [2, 320, 48, 48], P('section', 'dp')
- first_new: float32 [2, 1728], P('section', 'dp')
- second_new: float32 [2, 1728], P('section', 'dp')
- vectors_new: float32 [2, 1728], P('section', 'dp')
- grad_norm: float32 [], replicated
- loss_sum: float32 [], replicated
- weight_sum: float32 [], replicated
Inputs may be any that keep to these rules, and one draw needn't show every extreme that they name: `lengths`: one row of each micro-batch has length 512. The 32 positions of a row are distinct, increasing and below its length.
All inputs are finite; a program needn't handle non-finite values.
Results may differ from a plain program's by a relative error of at most 0.0052.
The roundings to bfloat16 on the way count: a program that leaves them out, or rounds other values in their place, can miss the bound.
Values may be sent and summed in bfloat16 or wider, within the bound.
No kernel may reach another device: no remote copies, remote signals or barrier semaphores. Data moves between devices by JAX's collectives and lax.ppermute only.
A program may use at most 576 MiB of HBM per device.

v0:
```python
import jax
import jax.numpy as jnp
from jax import lax
from jax.sharding import PartitionSpec as P

D = 768
HEADS = 12
HEAD_DIM = 64
BOT = 384
INV_H = 192
SEQ = 512
COUNT = 32
MICRO = 2
BLOCK = 48
STEP = 10
HALF = 384


HIGHEST = lax.Precision.HIGHEST
NORM_EPS = 1e-12
CLIP_NORM = 0.02
FIRST_DECAY = 0.9
STAT_DECAY = 0.99
MAT_RATE = 0.1
MAT_DECAY = 0.01
VEC_RATE = 0.05
VEC_SECOND = 0.999
VEC_EPS = 1e-08
VEC_DECAY = 0.01


def partner(block, axis, stride):
    count = lax.axis_size(axis)
    route = []
    for low in range(count):
        high = low | 1 << stride
        if high != low and high < count:
            route += [(low, high), (high, low)]
    return lax.ppermute(block, axis, route)


def from_behind(value, axis, steps):
    count = lax.axis_size(axis)
    first, last = (max(0, -steps), min(count, count - steps))
    return lax.ppermute(value, axis, [(source, source + steps) for source in range(first, last)])


def joined_2(value, axis, combine):
    everything = jax.tree.map(lambda part: lax.all_gather(part, axis), value)
    first = jax.tree.map(lambda part: part[0], everything)

    def turn(k, so_far):
        return combine(so_far, jax.tree.map(lambda part: part[k], everything))

    return lax.fori_loop(1, lax.axis_size(axis), turn, first)


def split_up(value, dim, length):
    dims = value.shape
    blocks = value.reshape(*dims[:dim], length, dims[dim] // length, *dims[dim + 1 :])
    return jnp.moveaxis(blocks, dim, 0)


def sum_at_owner(value, axis, dim):
    length = lax.axis_size(axis)
    blocks = lax.all_to_all(split_up(value, dim, length), axis, 0, 0, tiled=True)
    return jnp.sum(blocks.astype(jnp.float32), axis=0)


def matmul(left, right):
    return jnp.dot(left, right, preferred_element_type=jnp.float32)


def matmul_t(left, right):
    return lax.dot_general(
        left, right, (((left.ndim - 1,), (1,)), ((), ())), preferred_element_type=jnp.float32
    )


def inner_rows(left, right):
    return lax.dot_general(
        left, right, (((0,), (0,)), ((), ())), preferred_element_type=jnp.float32
    )


def when_valid(condition, function, *operands):

    def skipped(*inputs):
        return jax.tree.map(
            lambda leaf_item: jnp.zeros(leaf_item.shape, leaf_item.dtype), function(*inputs)
        )

    return lax.cond(condition, function, skipped, *operands)


def choose_leaves(condition, first_tree, second_tree):
    return jax.tree.map(
        lambda first_leaf, second_leaf: jnp.where(condition, first_leaf, second_leaf),
        first_tree,
        second_tree,
    )


def layer_norm(values, gain, shift):
    centered = values - jnp.mean(values, -1, keepdims=True)
    spread = jnp.mean(centered * centered, -1, keepdims=True)
    return centered * lax.rsqrt(spread + NORM_EPS) * gain + shift


def norm_back(incoming, values, gain):
    centered = values - jnp.mean(values, -1, keepdims=True)
    inverse = lax.rsqrt(jnp.mean(centered * centered, -1, keepdims=True) + NORM_EPS)
    normal_values = centered * inverse
    scaled = incoming * gain
    return inverse * (
        scaled
        - jnp.mean(scaled, -1, keepdims=True)
        - normal_values * jnp.mean(scaled * normal_values, -1, keepdims=True)
    )


def gelu_exact(values):
    return jax.nn.gelu(values, approximate=False)


def gelu_back(values, incoming):
    return jax.vjp(gelu_exact, values)[1](incoming)[0]


def to_blocks(matrix):
    rows_in, cols_in = matrix.shape
    return (
        matrix.reshape(rows_in // BLOCK, BLOCK, cols_in // BLOCK, BLOCK)
        .transpose(0, 2, 1, 3)
        .reshape(-1, BLOCK, BLOCK)
    )


def from_blocks(blocks, rows_in, cols_in):
    return (
        blocks.reshape(rows_in // BLOCK, cols_in // BLOCK, BLOCK, BLOCK)
        .transpose(0, 2, 1, 3)
        .reshape(rows_in, cols_in)
    )


def coupling_params(blocks, vector):
    half_count = HALF * INV_H // BLOCK**2
    return (
        from_blocks(blocks[:half_count], HALF, INV_H),
        vector[:INV_H],
        from_blocks(blocks[half_count:], INV_H, HALF),
        vector[INV_H:],
    )


def coupling_pack(weight_grads):
    blocks = jnp.concatenate([to_blocks(weight_grads[0]), to_blocks(weight_grads[2])])
    return (blocks, jnp.concatenate([weight_grads[1], weight_grads[3]]))


def branch_fwd(values, params):
    w_down, b_down, w_up, b_up = params
    low_in = values.astype(jnp.bfloat16)
    hidden = matmul(low_in, w_down) + b_down.astype(jnp.float32)
    active = gelu_exact(hidden).astype(jnp.bfloat16)
    return (matmul(active, w_up) + b_up.astype(jnp.float32), (low_in, hidden, active))


def branch_back(incoming, kept_state, params):
    w_down, b_down, w_up, b_up = params
    low_in, hidden, active = kept_state
    grad_low = incoming.astype(jnp.bfloat16)
    hidden_grad = gelu_back(hidden, matmul_t(grad_low, w_up)).astype(jnp.bfloat16)
    weight_grads = (
        inner_rows(low_in, hidden_grad),
        jnp.sum(hidden_grad.astype(jnp.float32), 0),
        inner_rows(active, grad_low),
        jnp.sum(grad_low.astype(jnp.float32), 0),
    )
    return (matmul_t(hidden_grad, w_down), weight_grads)


def split_heads(projected):
    query_rows = projected[:, :D].reshape(SEQ, HEADS, HEAD_DIM)
    key_rows = projected[:, D : 2 * D].reshape(SEQ, HEADS, HEAD_DIM)
    value_rows = projected[:, 2 * D :].reshape(SEQ, HEADS, HEAD_DIM)
    return (query_rows, key_rows, value_rows)


def block_scores(query_part, key_rows, length):
    scores = jnp.einsum(
        "qhd,khd->hqk", query_part, key_rows, preferred_element_type=jnp.float32
    ) * HEAD_DIM ** (-0.5)
    return jnp.where((jnp.arange(SEQ) < length)[None, None, :], scores, -1e30)


def attend_fwd(projected, length):
    block_rows = min(512, SEQ)
    query_rows, key_rows, value_rows = split_heads(projected)

    def one_block(block_index):
        scores = block_scores(query_rows, key_rows, length)
        highest = jnp.max(scores, -1, keepdims=True)
        exponent = jnp.exp(scores - highest)
        exp_total = jnp.sum(exponent, -1, keepdims=True)
        softmax_low = (exponent / exp_total).astype(jnp.bfloat16)
        mixed = jnp.einsum(
            "hqk,khd->qhd", softmax_low, value_rows, preferred_element_type=jnp.float32
        )
        return (
            mixed.reshape(block_rows, D).astype(jnp.bfloat16),
            (highest + jnp.log(exp_total))[..., 0],
        )

    mixed, log_total = lax.map(one_block, jnp.arange(SEQ // block_rows))
    return (mixed.reshape(SEQ, D), log_total)


def attend_back(projected, length, log_total, mixed_grad):
    block_rows = min(512, SEQ)
    query_rows, key_rows, value_rows = split_heads(projected)
    grad_heads = mixed_grad.reshape(SEQ, HEADS, HEAD_DIM)

    def one_block(carried, block_index):
        scores = block_scores(query_rows, key_rows, length)
        softmax_full = jnp.exp(scores - log_total[block_index][..., None])
        softmax_low = softmax_full.astype(jnp.bfloat16)
        weight_grad = jnp.einsum(
            "qhd,khd->hqk", grad_heads, value_rows, preferred_element_type=jnp.float32
        )
        score_grad = softmax_full * (
            weight_grad - jnp.sum(weight_grad * softmax_full, -1, keepdims=True)
        )
        score_grad = score_grad.astype(jnp.bfloat16)
        query_grad = jnp.einsum(
            "hqk,khd->qhd", score_grad, key_rows, preferred_element_type=jnp.float32
        ) * HEAD_DIM ** (-0.5)
        key_grad = jnp.einsum(
            "hqk,qhd->khd", score_grad, query_rows, preferred_element_type=jnp.float32
        ) * HEAD_DIM ** (-0.5)
        value_grad = jnp.einsum(
            "hqk,qhd->khd", softmax_low, grad_heads, preferred_element_type=jnp.float32
        )
        return ((carried[0] + key_grad, carried[1] + value_grad), query_grad)

    zero_heads = jnp.zeros((SEQ, HEADS, HEAD_DIM), jnp.float32)
    (key_grad, value_grad), query_grad = lax.scan(
        one_block, (zero_heads, zero_heads), jnp.arange(SEQ // block_rows)
    )
    return jnp.concatenate(
        [query_grad.reshape(SEQ, D), key_grad.reshape(SEQ, D), value_grad.reshape(SEQ, D)], -1
    )


def layer_fwd(hidden, lengths, weights):
    w_qkv, w_out, w_up, w_down, norm_gains, adapter = weights
    row_count = hidden.shape[0]
    flattened = hidden.reshape(-1, D)
    projected = (
        matmul(flattened.astype(jnp.bfloat16), w_qkv)
        .astype(jnp.bfloat16)
        .reshape(row_count, SEQ, 3 * D)
    )
    mixed, log_total = lax.map(
        lambda row_pair: attend_fwd(row_pair[0], row_pair[1]), (projected, lengths)
    )
    first_sum = flattened + matmul(mixed.reshape(-1, D), w_out)
    attended = layer_norm(first_sum, norm_gains[0], norm_gains[1])
    inner = matmul(attended.astype(jnp.bfloat16), w_up)
    summed = matmul(gelu_exact(inner).astype(jnp.bfloat16), w_down) + attended
    branch_out, branch_kept = branch_fwd(summed, adapter)
    second_sum = summed + branch_out
    result = layer_norm(second_sum, norm_gains[2], norm_gains[3]).reshape(hidden.shape)
    return (result, (projected, log_total, first_sum, inner, summed, branch_kept, second_sum))


def layer_back(incoming, kept_state, lengths, weights):
    w_qkv, w_out, w_up, w_down, norm_gains, adapter = weights
    projected, log_total, first_sum, inner, summed, branch_kept, second_sum = kept_state
    row_count = projected.shape[0]
    second_grad = norm_back(incoming.reshape(-1, D), second_sum, norm_gains[2])
    branch_grad, adapter_grads = branch_back(second_grad, branch_kept, adapter)
    summed_grad = second_grad + branch_grad
    inner_grad = gelu_back(inner, matmul_t(summed_grad.astype(jnp.bfloat16), w_down)).astype(
        jnp.bfloat16
    )
    attended_grad = summed_grad + matmul_t(inner_grad, w_up)
    start_grad = norm_back(attended_grad, first_sum, norm_gains[0])
    mixed_grad = (
        matmul_t(start_grad.astype(jnp.bfloat16), w_out)
        .astype(jnp.bfloat16)
        .reshape(row_count, SEQ, D)
    )
    projected_grad = lax.map(
        lambda entries: attend_back(entries[0], entries[1], entries[2], entries[3]),
        (projected, lengths, log_total, mixed_grad),
    )
    hidden_grad = start_grad + matmul_t(
        projected_grad.reshape(-1, 3 * D).astype(jnp.bfloat16), w_qkv
    )
    return (hidden_grad.reshape(row_count, SEQ, D), adapter_grads)


def first_fwd(embedded, norm_gains, coupling_one, coupling_two):
    started = layer_norm(embedded.reshape(-1, D), norm_gains[0], norm_gains[1])
    one_out, one_kept = branch_fwd(started[:, HALF:], coupling_one)
    left_half = started[:, :HALF] + one_out
    two_out, two_kept = branch_fwd(left_half, coupling_two)
    joined = jnp.concatenate([left_half, started[:, HALF:] + two_out], -1)
    return (joined.reshape(embedded.shape), (one_kept, two_kept))


def first_back(incoming, kept_state, coupling_one, coupling_two):
    incoming = incoming.reshape(-1, D)
    into_left, grads_two = branch_back(incoming[:, HALF:], kept_state[1], coupling_two)
    unused_grad, grads_one = branch_back(
        incoming[:, :HALF] + into_left, kept_state[0], coupling_one
    )
    return (grads_one, grads_two)


def last_fwd(hidden, norm_gains, coupling_one, coupling_two):
    flattened = hidden.reshape(-1, D)
    two_out, two_kept = branch_fwd(flattened[:, :HALF], coupling_two)
    right_half = flattened[:, HALF:] - two_out
    one_out, one_kept = branch_fwd(right_half, coupling_one)
    restored = jnp.concatenate([flattened[:, :HALF] - one_out, right_half], -1)
    return (layer_norm(restored, norm_gains[0], norm_gains[1]), (restored, one_kept, two_kept))


def last_back(incoming, kept_state, norm_gains, coupling_one, coupling_two):
    restored, one_kept, two_kept = kept_state
    restored_grad = norm_back(incoming, restored, norm_gains[0])
    left_grad = restored_grad[:, :HALF]
    into_right, grads_one = branch_back(-left_grad, one_kept, coupling_one)
    right_grad = restored_grad[:, HALF:] + into_right
    into_left, grads_two = branch_back(-right_grad, two_kept, coupling_two)
    return (jnp.concatenate([left_grad + into_left, right_grad], -1), grads_one, grads_two)


def head_scores(gathered_rows, embed_table, goal_index):
    logits = matmul_t(gathered_rows, embed_table)
    highest = jnp.max(logits, -1)
    exp_total = jnp.sum(jnp.exp(logits - highest[:, None]), -1)
    onehot = jnp.arange(embed_table.shape[0])[None, :] == goal_index[:, None]
    return (logits, highest, exp_total, jnp.sum(jnp.where(onehot, logits, 0.0), -1))


def combine_stats(earlier, later):
    highest = jnp.maximum(earlier[0], later[0])
    exp_total = earlier[1] * jnp.exp(earlier[0] - highest) + later[1] * jnp.exp(later[0] - highest)
    return (highest, exp_total, earlier[2] + later[2])


def shards(
    token_ids,
    lengths,
    positions,
    targets,
    loss_weights,
    embed_table,
    pos_table,
    norm_params,
    base_qkv,
    base_out,
    base_up,
    base_down,
    master,
    momentum,
    stat_left,
    stat_right,
    root_left,
    root_right,
    vectors,
    vec_first,
    vec_second,
):
    first_section = lax.axis_index("section") == 0
    data_index = lax.axis_index("dp")
    vocab_rows = embed_table.shape[0]
    local_rows = token_ids.shape[1]
    adapter_count = D * BOT // BLOCK**2
    split_at = 2 * adapter_count
    own_blocks, own_vector = (
        lax.all_gather(master[0].astype(jnp.bfloat16), "dp", axis=0, tiled=True),
        lax.all_gather(vectors[0].astype(jnp.bfloat16), "dp", axis=0, tiled=True),
    )
    other_blocks, other_vector = partner(
        (own_blocks[split_at:], own_vector[BOT + D :]), "section", 0
    )
    adapter = (
        from_blocks(own_blocks[:adapter_count], D, BOT),
        own_vector[:BOT],
        from_blocks(own_blocks[adapter_count:split_at], BOT, D),
        own_vector[BOT : BOT + D],
    )
    own_coupling = coupling_params(own_blocks[split_at:], own_vector[BOT + D :])
    other_coupling = coupling_params(other_blocks, other_vector)
    coupling_one = choose_leaves(first_section, own_coupling, other_coupling)
    coupling_two = choose_leaves(first_section, other_coupling, own_coupling)
    section_weights = (
        base_qkv[0],
        base_out[0],
        base_up[0],
        base_down[0],
        norm_params[0, 2:],
        adapter,
    )
    edge_gains = norm_params[0, :2]
    all_ids, all_targets, all_weights = (
        lax.all_gather(token_ids, "dp", axis=1, tiled=True),
        lax.all_gather(targets, "dp", axis=1, tiled=True),
        lax.all_gather(loss_weights, "dp", axis=1, tiled=True),
    )
    weight_sum = jnp.sum(all_weights.astype(jnp.float32))
    ordered = jnp.transpose(all_ids, (1, 0, 2)).reshape(-1)
    columns = lax.all_to_all(embed_table, "dp", split_axis=1, concat_axis=0, tiled=True)
    picked = jnp.take(columns, ordered, axis=0)
    embedded = lax.all_to_all(picked, "dp", split_axis=0, concat_axis=1, tiled=True).astype(
        jnp.float32
    )
    embedded = embedded.reshape(local_rows, MICRO, SEQ, D).transpose(1, 0, 2, 3) + pos_table.astype(
        jnp.float32
    )
    zero_rows = jnp.zeros((local_rows, SEQ, D), jnp.float32)
    received = zero_rows.astype(jnp.bfloat16)
    arrived_grad = zero_rows
    loss_part = jnp.zeros((), jnp.float32)
    adapter_grads = jax.tree.map(
        jnp.zeros_like, jax.tree.map(lambda leaf_item: leaf_item.astype(jnp.float32), adapter)
    )
    zero_coupling = jax.tree.map(
        lambda leaf_item: jnp.zeros(leaf_item.shape, jnp.float32), own_coupling
    )
    grads_first, grads_second = (zero_coupling, zero_coupling)
    kept_layers, kept_starts = ([], [])
    row_index = jnp.arange(local_rows)[:, None]
    for clock_tick in range(MICRO + 2):
        front_batch = min(clock_tick, MICRO - 1)
        middle_batch = max(min(clock_tick - 1, MICRO - 1), 0)
        rear_batch = max(min(clock_tick - 2, MICRO - 1), 0)
        forward_ok = jnp.where(
            first_section, clock_tick < MICRO, (clock_tick >= 1) & (clock_tick <= MICRO)
        )
        backward_ok = jnp.where(
            first_section,
            (clock_tick >= 2) & (clock_tick <= MICRO + 1),
            (clock_tick >= 1) & (clock_tick <= MICRO),
        )
        start_out, start_kept = when_valid(
            first_section & (clock_tick < MICRO),
            first_fwd,
            embedded[front_batch],
            edge_gains,
            coupling_one,
            coupling_two,
        )
        layer_in = jnp.where(first_section, start_out, received.astype(jnp.float32))
        forward_lengths = jnp.where(first_section, lengths[front_batch], lengths[middle_batch])
        layer_out, layer_kept = when_valid(
            forward_ok, layer_fwd, layer_in, forward_lengths, section_weights
        )
        kept_layers.append(layer_kept)
        kept_starts.append(start_kept)
        if clock_tick < MICRO:
            received = from_behind(layer_out.astype(jnp.bfloat16), "section", 1)
        head_grad = zero_rows
        if 1 <= clock_tick <= MICRO:
            head_ok = jnp.logical_not(first_section)
            normed, last_kept = when_valid(
                head_ok, last_fwd, layer_out, edge_gains, coupling_one, coupling_two
            )
            chosen = normed.reshape(local_rows, SEQ, D)[row_index, positions[middle_batch]].reshape(
                -1, D
            )
            gathered_rows = lax.all_gather(chosen.astype(jnp.bfloat16), "dp", axis=0, tiled=True)
            goal_index = all_targets[middle_batch].reshape(-1) - data_index * vocab_rows
            row_weights = all_weights[middle_batch].reshape(-1).astype(jnp.float32)
            logits, highest, exp_total, target_logit = when_valid(
                head_ok, head_scores, gathered_rows, embed_table, goal_index
            )
            highest, exp_total, target_logit = joined_2(
                (highest, exp_total, target_logit), "dp", combine_stats
            )

            def head_grads(logits, highest, exp_total, target_logit):
                log_total = highest + jnp.log(exp_total)
                losses = row_weights * (log_total - target_logit)
                own_losses = lax.dynamic_slice_in_dim(
                    losses, data_index * chosen.shape[0], chosen.shape[0], 0
                )
                onehot = (jnp.arange(vocab_rows)[None, :] == goal_index[:, None]).astype(
                    jnp.float32
                )
                scaled = (row_weights / weight_sum)[:, None] * (
                    jnp.exp(logits - log_total[:, None]) - onehot
                )
                return (jnp.sum(own_losses), scaled.astype(jnp.bfloat16))

            loss_add, logits_grad = when_valid(
                head_ok, head_grads, logits, highest, exp_total, target_logit
            )
            loss_part = loss_part + loss_add
            row_count = chosen.shape[0] * lax.axis_size("dp")

            def compute(grad_rows):
                return matmul(grad_rows, embed_table)

            chosen_grad = sum_at_owner(
                lax.cond(
                    head_ok,
                    compute,
                    lambda grad_rows: jnp.zeros((row_count, D), jnp.float32),
                    logits_grad,
                ).astype(jnp.bfloat16),
                "dp",
                0,
            )
            normed_grad = zero_rows.at[row_index, positions[middle_batch]].add(
                chosen_grad.reshape(local_rows, COUNT, D)
            )
            head_flat, last_one, last_two = when_valid(
                head_ok,
                last_back,
                normed_grad.reshape(-1, D),
                last_kept,
                edge_gains,
                coupling_one,
                coupling_two,
            )
            head_grad = head_flat.reshape(local_rows, SEQ, D)
            grads_first = jax.tree.map(jnp.add, grads_first, last_one)
            grads_second = jax.tree.map(jnp.add, grads_second, last_two)
        older = kept_layers[clock_tick - 2] if clock_tick >= 2 else kept_layers[clock_tick]
        selected = choose_leaves(first_section, older, kept_layers[clock_tick])
        backward_lengths = jnp.where(first_section, lengths[rear_batch], lengths[middle_batch])
        output_grad = jnp.where(first_section, arrived_grad, head_grad)

        def run_back(incoming, kept_state, lengths_now):
            return layer_back(incoming, kept_state, lengths_now, section_weights)

        input_grad, layer_grads = when_valid(
            backward_ok, run_back, output_grad, selected, backward_lengths
        )
        adapter_grads = jax.tree.map(jnp.add, adapter_grads, layer_grads)
        if clock_tick >= 2:
            start_one, start_two = when_valid(
                first_section & backward_ok,
                first_back,
                input_grad,
                kept_starts[clock_tick - 2],
                coupling_one,
                coupling_two,
            )
            grads_first = jax.tree.map(jnp.add, grads_first, start_one)
            grads_second = jax.tree.map(jnp.add, grads_second, start_two)
        if 1 <= clock_tick <= MICRO:
            arrived_grad = from_behind(input_grad.astype(jnp.bfloat16), "section", -1).astype(
                jnp.float32
            )
    own_coupling_grad = choose_leaves(first_section, grads_first, grads_second)
    other_coupling_grad = choose_leaves(first_section, grads_second, grads_first)
    own_pack_blocks, own_pack_vector = coupling_pack(own_coupling_grad)
    other_pack_blocks, other_pack_vector = coupling_pack(other_coupling_grad)
    came_blocks, came_vector = (
        partner(other_pack_blocks.astype(jnp.bfloat16), "section", 0).astype(
            other_pack_blocks.dtype
        ),
        partner(other_pack_vector.astype(jnp.bfloat16), "section", 0).astype(
            other_pack_vector.dtype
        ),
    )
    section_blocks = jnp.concatenate(
        [to_blocks(adapter_grads[0]), to_blocks(adapter_grads[2]), own_pack_blocks + came_blocks]
    )
    section_vector = jnp.concatenate(
        [adapter_grads[1], adapter_grads[3], own_pack_vector + came_vector]
    )
    grad_blocks, grad_vector = (
        sum_at_owner(section_blocks.astype(jnp.bfloat16), "dp", 0),
        sum_at_owner(section_vector.astype(jnp.bfloat16), "dp", 0),
    )
    squares = jnp.sum(grad_blocks * grad_blocks) + jnp.sum(grad_vector * grad_vector)
    squares, loss_sum = lax.psum((squares, loss_part), ("dp", "section"))
    grad_norm = jnp.sqrt(squares)
    factor = CLIP_NORM / jnp.maximum(grad_norm, CLIP_NORM)
    clipped = grad_blocks * factor
    clipped_vector = grad_vector * factor
    momentum_new = FIRST_DECAY * momentum[0] + (1.0 - FIRST_DECAY) * clipped
    left_new = STAT_DECAY * stat_left[0] + (1.0 - STAT_DECAY) * jnp.einsum(
        "nij,nkj->nik", clipped, clipped, precision=HIGHEST
    )
    right_new = STAT_DECAY * stat_right[0] + (1.0 - STAT_DECAY) * jnp.einsum(
        "nji,njk->nik", clipped, clipped, precision=HIGHEST
    )
    direction = jnp.einsum("nij,njk->nik", root_left[0], momentum_new, precision=HIGHEST)
    direction = jnp.einsum("nij,njk->nik", direction, root_right[0], precision=HIGHEST)
    master_new = master[0] - MAT_RATE * (direction + MAT_DECAY * master[0])
    first_new = FIRST_DECAY * vec_first[0] + (1.0 - FIRST_DECAY) * clipped_vector
    second_new = VEC_SECOND * vec_second[0] + (1.0 - VEC_SECOND) * clipped_vector * clipped_vector
    corrected_first = first_new / (1.0 - FIRST_DECAY**STEP)
    corrected_second = second_new / (1.0 - VEC_SECOND**STEP)
    vectors_new = vectors[0] - VEC_RATE * (
        corrected_first / (jnp.sqrt(corrected_second) + VEC_EPS) + VEC_DECAY * vectors[0]
    )
    return (
        clipped[None],
        momentum_new[None],
        left_new[None],
        right_new[None],
        master_new[None],
        master_new.astype(jnp.bfloat16)[None],
        first_new[None],
        second_new[None],
        vectors_new[None],
        grad_norm,
        loss_sum,
        weight_sum,
    )


def solution(mesh):
    return jax.shard_map(
        shards,
        mesh=mesh,
        in_specs=(
            P(None, "dp", None),
            P(None, "dp"),
            P(None, "dp", None),
            P(None, "dp", None),
            P(None, "dp", None),
            P("dp", None),
            P(),
            P("section", None, None),
            P("section", None, None),
            P("section", None, None),
            P("section", None, None),
            P("section", None, None),
            P("section", "dp", None, None),
            P("section", "dp", None, None),
            P("section", "dp", None, None),
            P("section", "dp", None, None),
            P("section", "dp", None, None),
            P("section", "dp", None, None),
            P("section", "dp"),
            P("section", "dp"),
            P("section", "dp"),
        ),
        out_specs=(
            P("section", "dp", None, None),
            P("section", "dp", None, None),
            P("section", "dp", None, None),
            P("section", "dp", None, None),
            P("section", "dp", None, None),
            P("section", "dp", None, None),
            P("section", "dp"),
            P("section", "dp"),
            P("section", "dp"),
            P(),
            P(),
            P(),
        ),
        check_vma=False,
    )
```

profile of v0, /device:TPU:0, one launch (start us, length us, event | category | flops | bytes accessed | tf_op | source)
XLA Modules:
  0.0 1767.0 jit_solution(17699731332412866030)
XLA Ops:
  7.2 15.2 copy.531
  22.4 8.5 all-to-all-start
  31.7 265.5 %all_gather.57 = s32[2,16,512]{2,0,1:T(2,128)S(1)} all-gather(s32[2,1,512]{2,0,1:T(2,128)S(1)} %copy.530), channel_id=1, replica_groups=mesh['dp'=16,'section'=2] {'dp'}, dimensions={1}, use_global_device_ids=true | all-gather | bytes 69632 | tf_op jit(solution)/shard_map/all_gather | solution.py:412
  297.4 26.8 %copy.532 = bf16[16,7472,48]{2,1,0:T(8,128)(2,1)} copy(bf16[16,7472,48]{1,2,0:T(8,128)(2,1)} %bitcast.86) | data formatting | bytes 22953984 | tf_op jit(solution)/shard_map/all_to_all | solution.py:418
  324.2 68.6 %gather_fusion = bf16[16384,48]{1,0:T(8,128)(2,1)} fusion(bf16[119552,48]{1,0:T(8,128)(2,1)} %bitcast.573, s32[16384]{0:T(1024)S(1)} %broadcast_clamp_fusion), kind=kCustom, calls=%fused_computation | custom fusion | bytes 3211264 | tf_op jit(solution)/shard_map/jit(_take)/gather | solution.py:419
  397.8 56.1 %all-to-all-start.1 = ((bf16[16,1024,48]{1,2,0:T(8,128)(2,1)}), bf16[16,1024,48]{1,2,0:T(8,128)(2,1)}, u32[]{:S(2)}, u32[]{:S(2)}) async-start(bf16[16,1024,48]{1,2,0:T(8,128)(2,1)} %broadcast_select_fusion.4), calls=%async_computation.1 | async-start | bytes 3145728 | tf_op jit(solution)/shard_map/all_to_all | solution.py:420
  455.5 51.5 %all-reduce.2 = bf16[1728]{0:T(1024)(128)(2,1)S(1)} all-reduce(bf16[1728]{0:T(1024)(128)(2,1)S(1)} %dynamic-update-slice), channel_id=2, replica_groups=mesh['dp'=16,'section'=2] {'dp'}, use_global_device_ids=true, to_apply=%add.2 | all-reduce | flops 1728 | bytes 6912
  515.4 37.7 %all_gather.62 = s32[2,16,32]{2,0,1:T(2,128)S(1)} all-gather(s32[2,1,32]{2,0,1:T(2,128)S(1)} %bitcast.692), channel_id=1, replica_groups=mesh['dp'=16,'section'=2] {'dp'}, dimensions={1}, use_global_device_ids=true | all-gather | bytes 4352 | tf_op jit(solution)/shard_map/all_gather | solution.py:413
  556.3 35.7 %all_gather.60 = s32[2,16,32]{2,0,1:T(2,128)S(1)} all-gather(s32[2,1,32]{2,0,1:T(2,128)S(1)} %bitcast.693), channel_id=1, replica_groups=mesh['dp'=16,'section'=2] {'dp'}, dimensions={1}, use_global_device_ids=true | all-gather | bytes 4352 | tf_op jit(solution)/shard_map/all_gather | solution.py:414
  613.9 5.6 reshape.1352
  619.6 5.3 broadcast_add_fusion
  625.0 9.4 conditional.19
  635.9 79.5 %conditional.20 = (bf16[1,512,768]{2,1,0:T(8,128)(2,1)}, f32[1,1,12,512]{3,2,1,0:T(8,128)}, f32[512,768]{1,0:T(8,128)}, f32[512,3072]{1,0:T(8,128)}, bf16[512,76...) conditional(s32[]{:T(128)} %convert_element_type.662, ...), branch_computations={%region_8.9_spmd, %region_9.16_spmd} | conditional | flops 8822977536 | bytes 148597440 | solution.py:93
  640.4 4.5 convolution_convert_fusion
  656.1 4.6 fusion.98
  663.3 4.5 fusion.116
  671.9 8.2 fusion.121
  680.1 18.8 %fusion.757 = (bf16[512,768]{1,0:T(8,128)(2,1)}, f32[512,768]{1,0:T(8,128)S(1)}) fusion(f32[768]{0:T(1024)S(1)} %copy-done.194, f32[768]{0:T(1024)S(1)} %copy-done.195, f32[512]{0:T(512)S(1)} %add_rsqrt_fusion.3, f32[512,768]{1,0:T(8,128)} %get-tuple-element.3112, f32[512]{0:T(512)S(1)} %broadcast_multiply_fusion.3, bf16[3072,768]{1,0:T(8,128)(2,1)S(1)} %bitcast.705, ...), kind=kOutput, calls=%fused_computation.1340 | convolution fusion | flops 2520514560 | bytes 14952448 | tf_op jit(solution)/shard_map/cond/branch_1_fun/dot_general | solution.py:71
  698.9 4.3 fusion.120
  710.9 4.3 copy.668
  722.6 15.0 conditional.18
  737.6 4.7 convolution_convert_fusion.4
  761.6 5.4 fusion.594
  767.1 15.8 fusion.779
  788.8 5.8 conditional.21
  796.0 42.1 %all-gather.9 = bf16[512,768]{1,0:T(8,128)(2,1)S(1)} all-gather(bf16[32,768]{1,0:T(8,128)(2,1)S(1)} %gather_fusion.1), channel_id=11, replica_groups=mesh['dp'=16,'section'=2] {'dp'}, dimensions={0}, use_global_device_ids=true | all-gather | bytes 835584 | tf_op jit(solution)/shard_map/all_gather | solution.py:477
  838.1 8.3 conditional.22
  838.1 7.4 broadcast.2753
  846.4 36.1 %all-gather.11 = f32[16,1,512]{2,1,0:T(1,128)S(1)} all-gather(f32[1,1,512]{2,1,0:T(1,128)} %bitcast.129), channel_id=4, replica_groups=mesh['dp'=16,'section'=2] {'dp'}, dimensions={0}, use_global_device_ids=true | all-gather | bytes 34816 | tf_op jit(solution)/shard_map/all_gather | solution.py:49
  882.5 37.4 %all-gather.12 = f32[16,1,512]{2,1,0:T(1,128)S(1)} all-gather(f32[1,1,512]{2,1,0:T(1,128)S(1)} %bitcast.688), channel_id=5, replica_groups=mesh['dp'=16,'section'=2] {'dp'}, dimensions={0}, use_global_device_ids=true | all-gather | bytes 34816 | tf_op jit(solution)/shard_map/all_gather | solution.py:49
  919.9 35.8 %all-gather.13 = f32[16,1,512]{2,1,0:T(1,128)S(1)} all-gather(f32[1,1,512]{2,1,0:T(1,128)S(1)} %bitcast.689), channel_id=6, replica_groups=mesh['dp'=16,'section'=2] {'dp'}, dimensions={0}, use_global_device_ids=true | all-gather | bytes 34816 | tf_op jit(solution)/shard_map/all_gather | solution.py:49
  960.9 4.3 all-to-all-start.2
  967.1 19.4 %conditional.27 = (f32[1,512,768]{2,1,0:T(8,128)}, f32[1,1,12,512]{3,2,1,0:T(8,128)S(1)}, f32[512,768]{1,0:T(8,128)}, f32[512,3072]{1,0:T(8,128)}, bf16[512,768]...) conditional(s32[]{:T(128)} %convert_element_type.661, ...), branch_computations={%region_65.66_spmd, %region_66.73_spmd} | conditional | flops 8822584320 | bytes 162004544 | solution.py:93
  987.2 5.0 conditional.28
  993.8 45.1 %all-gather.10 = bf16[512,768]{1,0:T(8,128)(2,1)S(1)} all-gather(bf16[32,768]{1,0:T(8,128)(2,1)S(1)} %gather_fusion.2), channel_id=12, replica_groups=mesh['dp'=16,'section'=2] {'dp'}, dimensions={0}, use_global_device_ids=true | all-gather | bytes 835584 | tf_op jit(solution)/shard_map/all_gather | solution.py:477
  1038.9 7.9 conditional.29
  1038.9 7.4 broadcast.2973
  1046.8 35.9 %all-gather.14 = f32[16,1,512]{2,1,0:T(1,128)S(1)} all-gather(f32[1,1,512]{2,1,0:T(1,128)} %bitcast.144), channel_id=8, replica_groups=mesh['dp'=16,'section'=2] {'dp'}, dimensions={0}, use_global_device_ids=true | all-gather | bytes 34816 | tf_op jit(solution)/shard_map/all_gather | solution.py:49
  1082.7 37.5 %all-gather.15 = f32[16,1,512]{2,1,0:T(1,128)S(1)} all-gather(f32[1,1,512]{2,1,0:T(1,128)S(1)} %bitcast.690), channel_id=9, replica_groups=mesh['dp'=16,'section'=2] {'dp'}, dimensions={0}, use_global_device_ids=true | all-gather | bytes 34816 | tf_op jit(solution)/shard_map/all_gather | solution.py:49
  1120.2 35.8 %all-gather.16 = f32[16,1,512]{2,1,0:T(1,128)S(1)} all-gather(f32[1,1,512]{2,1,0:T(1,128)S(1)} %bitcast.691), channel_id=10, replica_groups=mesh['dp'=16,'section'=2] {'dp'}, dimensions={0}, use_global_device_ids=true | all-gather | bytes 34816 | tf_op jit(solution)/shard_map/all_gather | solution.py:49
  1164.7 4.3 all-to-all-start.3
  1176.7 4.2 conditional.25
  1182.2 9.3 conditional.26
  1192.9 7.5 fusion.789
  1203.7 4.7 conditional.32
  1208.4 177.8 %collective-permute-done.4 = bf16[1,512,768]{2,1,0:T(8,128)(2,1)} collective-permute-done((bf16[1,512,768]{2,1,0:T(8,128)(2,1)}, bf16[1,512,768]{2,1,0:T(8,128)(2,1)}, u32[]{:S(2)}, u32[]{:S(2)}) %collective-permute-start.4) | collective-permute-done | bytes 786464 | tf_op jit(solution)/shard_map/ppermute | solution.py:45
  1397.9 26.2 %fusion.742 = (f32[512]{0:T(512)S(1)}, f32[512]{0:T(512)S(1)}, f32[512,768]{1,0:T(8,128)}) fusion(f32[512]{0:T(512)S(1)} %add_rsqrt_fusion.14, f32[512,768]{1,0:T(8,128)} %copy-done.47, f32[512]{0:T(512)S(1)} %broadcast_multiply_fusion.26, f32[768]{0:T(1024)S(1)} %copy-done.192, f32[512,768]{1,0:T(8,128)} %convolution_add_fusion.26, ...), kind=kOutput, calls=%fused_computation.1329 | convolution fusion | flops 4949801984 | bytes 26749952 | tf_op jit(solution)/shard_map/cond/branch_1_fun/dot_general | solution.py:75
  1430.6 8.1 fusion.572
  1438.7 11.5 multiply_reduce_fusion.22
  1451.3 7.2 multiply_convert_fusion.8
  1469.3 6.9 conditional.34
  1482.1 19.7 %collective-permute-done.5 = bf16[1,512,768]{2,1,0:T(8,128)(2,1)} collective-permute-done((bf16[1,512,768]{2,1,0:T(8,128)(2,1)}, bf16[1,512,768]{2,1,0:T(8,128)(2,1)}, u32[]{:S(2)}, u32[]{:S(2)}) %collective-permute-start.5) | collective-permute-done | bytes 786464 | tf_op jit(solution)/shard_map/ppermute | solution.py:45
  1509.8 79.3 %conditional.33 = (f32[1,512,768]{2,1,0:T(8,128)}, f32[768,384]{1,0:T(8,128)}, f32[384]{0:T(512)S(1)}, f32[384,768]{1,0:T(8,128)}, f32[768]{0:T(1024)S(1)}) conditional(s32[]{:T(128)} %convert_element_type.662, () %tuple.283, (pred[512,768]{1,0:T(32,128)(4,1)S(1)}, f32[512,768]{1,0:T(8,128)S(1)}, f32[512,768]{1,0:T(8,128)S(1)}, ...), branch_computations={%region_111.112_spmd, %region_112.124_spmd} | conditional | flops 10676994048 | bytes 277900320 | solution.py:93
  1516.4 28.7 %fusion.740 = (f32[512]{0:T(512)S(1)}, f32[512]{0:T(512)S(1)}, f32[512,768]{1,0:T(8,128)}) fusion(f32[512]{0:T(512)S(1)} %add_rsqrt_fusion.13, f32[512,768]{1,0:T(8,128)S(1)} %copy-done.41, f32[512]{0:T(512)S(1)} %broadcast_multiply_fusion.23, f32[768]{0:T(1024)S(1)} %get-tuple-element.2721, f32[512,768]{1,0:T(8,128)} %convolution_add_fusion.25, ...), kind=kOutput, calls=%fused_computation.1327 | convolution fusion | flops 4949801984 | bytes 28322816 | tf_op jit(solution)/shard_map/cond/branch_1_fun/dot_general | solution.py:75
  1545.2 4.7 convolution_convert_fusion.3
  1562.7 7.3 multiply_reduce_fusion.17
  1570.0 7.1 multiply_convert_fusion.5
  1589.1 13.0 conditional.35
  1636.3 6.8 all-to-all-start.5
  1650.8 9.3 reshape.1511
  1660.1 7.0 all-to-all-start.4
  1667.8 30.8 %all-to-all-done.4 = bf16[16,2,23040]{2,1,0:T(2,128)(2,1)S(1)} async-done(((bf16[16,2,23040]{2,1,0:T(2,128)(2,1)}), bf16[16,2,23040]{2,1,0:T(2,128)(2,1)S(1)}, u32[]{:S(2)}, u32[]{:S(2)}) %all-to-all-start.4) | async-done | bytes 1474592 | tf_op jit(solution)/shard_map/all_to_all | solution.py:66
  1698.5 4.9 reshape.1512
  1708.5 42.3 %all-reduce.3 = (f32[]{:T(128)}, f32[]{:T(128)}) all-reduce(f32[]{:T(128)S(6)} %add.1095, f32[]{:T(128)S(6)} %add.1106), channel_id=1, replica_groups=mesh['dp'=16,'section'=2] {'dp','section'}, use_global_device_ids=true, to_apply=%region_142.143 | all-reduce | flops 2 | bytes 16 | tf_op jit(solution)/shard_map/psum | solution.py:585
  (890 shorter events, 344.0 us)
Async XLA Ops:
  7.2 1748.9 %copy-start = (f32[1,20,48,48]{3,2,1,0:T(8,128)S(1)}, f32[1,20,48,48]{3,2,1,0:T(8,128)}, u32[]{:S(2)}) copy-start(f32[1,20,48,48]{3,2,1,0:T(8,128)} %param.77) | copy-start | bytes 552964
  22.4 275.0 %all-to-all-start = ((bf16[7472,16,48]{0,2,1:T(8,128)(2,1)}), bf16[7472,16,48]{0,2,1:T(8,128)(2,1)}, u32[]{:S(2)}, u32[]{:S(2)}) async-start(bf16[7472,16,48]{0,2,1:T(8,128)(2,1)} %bitcast.576), calls=%async_computation | async-start | bytes 23199744 | tf_op jit(solution)/shard_map/all_to_all | solution.py:418
  30.9 562.3 %all-gather.19.cloned.1.call-start = ((), (), s32[]{:S(2)}) async-start(), calls=%async_computation.6 | async-start | bytes 4177920 | tf_op jit(solution)/shard_map/all_gather | solution.py:386
  392.8 61.2 %copy-start.230 = (u32[32]{0:T(128)S(1)}, u32[32]{0:T(128)}, u32[]{:S(2)}) copy-start(u32[32]{0:T(128)} %constant.1922) | copy-start | bytes 388
  392.8 62.4 %copy-start.221 = (f32[1,108]{1,0:T(1,128)S(1)}, f32[1,108]{1,0:T(1,128)}, u32[]{:S(2)}) copy-start(f32[1,108]{1,0:T(1,128)} %param.79) | copy-start | bytes 1300
  392.8 114.3 %copy-start.202 = (s32[2,1]{0,1:T(1,128)S(1)}, s32[2,1]{0,1:T(1,128)}, u32[]{:S(2)}) copy-start(s32[2,1]{0,1:T(1,128)} %param.62) | copy-start | bytes 28
  392.8 117.6 %copy-start.125 = (bf16[512,768]{1,0:T(8,128)(2,1)S(1)}, bf16[512,768]{1,0:T(8,128)(2,1)}, u32[]{:S(2)}) copy-start(bf16[512,768]{1,0:T(8,128)(2,1)} %param.67) | copy-start | bytes 2359300
  396.4 115.4 %slice-start.3 = ((f32[1,6,768]{2,0,1:T(1,128)}), f32[1,2,768]{2,0,1:T(1,128)S(1)}, s32[]{:S(2)}) async-start(f32[1,6,768]{2,0,1:T(1,128)} %param.68), calls=%async_computation.10 | async-start | bytes 12288 | tf_op jit(solution)/shard_map/slice | solution.py:410
  396.4 116.0 %slice-start.4 = ((f32[1,6,768]{2,0,1:T(1,128)}), f32[1,4,768]{2,0,1:T(1,128)S(1)}, s32[]{:S(2)}) async-start(f32[1,6,768]{2,0,1:T(1,128)} %param.68), calls=%async_computation.11 | async-start | bytes 24576 | tf_op jit(solution)/shard_map/slice | solution.py:407
  396.4 119.0 %copy-start.203 = (s32[2,1,32]{2,1,0:T(1,128)S(1)}, s32[2,1,32]{2,1,0:T(1,128)}, u32[]{:S(2)}) copy-start(s32[2,1,32]{2,1,0:T(1,128)} %param.64) | copy-start | bytes 772
  396.4 158.7 %copy-start.205 = (s32[2,1,32]{2,1,0:T(1,128)S(1)}, s32[2,1,32]{2,1,0:T(1,128)}, u32[]{:S(2)}) copy-start(s32[2,1,32]{2,1,0:T(1,128)} %param.63) | copy-start | bytes 772
  396.4 159.8 %copy-start.204 = (s32[2,1,32]{2,1,0:T(1,128)S(1)}, s32[2,1,32]{2,1,0:T(1,128)}, u32[]{:S(2)}) copy-start(s32[2,1,32]{2,1,0:T(1,128)} %param.65) | copy-start | bytes 772
  397.8 212.5 %all-to-all-start.1 = ((bf16[16,1024,48]{1,2,0:T(8,128)(2,1)}), bf16[16,1024,48]{1,2,0:T(8,128)(2,1)}, u32[]{:S(2)}, u32[]{:S(2)}) async-start(bf16[16,1024,48]{1,2,0:T(8,128)(2,1)} %broadcast_select_fusion.4), calls=%async_computation.1 | async-start | bytes 3145728 | tf_op jit(solution)/shard_map/all_to_all | solution.py:420
  507.0 84.9 %collective-permute-start.1 = (bf16[576]{0:T(1024)(128)(2,1)S(1)}, bf16[576]{0:T(1024)(128)(2,1)S(1)}, u32[]{:S(2)}, u32[]{:S(2)}) collective-permute-start(bf16[576]{0:T(1024)(128)(2,1)S(1)} %slice_reduce_fusion.29), channel_id=1, source_target_pairs={{0,1},{1,0},{2,3},{3,2},{4,5},{5,4},{6,7},{7,6},{8,9},{9,8},{10,11... | collective-permute-start | bytes 3464 | tf_op jit(solution)/shard_map/ppermute | solution.py:39
  591.9 126.1 %copy-start.138 = (s32[2,16,32]{2,0,1:T(2,128)}, s32[2,16,32]{2,0,1:T(2,128)S(1)}, u32[]{:S(2)}) copy-start(s32[2,16,32]{2,0,1:T(2,128)S(1)} %all_gather.60) | copy-start | bytes 12292
  595.0 9.9 collective-permute-start
  609.9 178.9 %copy-start.57 = (bf16[384,192]{0,1:T(8,128)(2,1)}, bf16[384,192]{0,1:T(8,128)(2,1)S(1)}, u32[]{:S(2)}) copy-start(bf16[384,192]{0,1:T(8,128)(2,1)S(1)} %select_n.498) | copy-start | bytes 442372
  610.3 178.5 %copy-start.52 = (bf16[192,384]{1,0:T(8,128)(2,1)}, bf16[192,384]{1,0:T(8,128)(2,1)S(1)}, u32[]{:S(2)}) copy-start(bf16[192,384]{1,0:T(8,128)(2,1)S(1)} %select_n.503) | copy-start | bytes 442372
  680.0 18.8 %copy-start.156 = (bf16[768]{0:T(1024)(128)(2,1)S(1)}, bf16[768]{0:T(1024)(128)(2,1)}, u32[]{:S(2)}) copy-start(bf16[768]{0:T(1024)(128)(2,1)} %get-tuple-element.1334) | copy-start | bytes 4612 | tf_op jit(solution)/shard_map/cond
  680.0 18.8 %copy-start.173 = (bf16[384]{0:T(512)(128)(2,1)S(1)}, bf16[384]{0:T(512)(128)(2,1)}, u32[]{:S(2)}) copy-start(bf16[384]{0:T(512)(128)(2,1)} %get-tuple-element.1332) | copy-start | bytes 2308 | tf_op jit(solution)/shard_map/cond
  680.1 18.8 %copy-start.35 = (bf16[768,384]{1,0:T(8,128)(2,1)S(1)}, bf16[768,384]{1,0:T(8,128)(2,1)}, u32[]{:S(2)}) copy-start(bf16[768,384]{1,0:T(8,128)(2,1)} %get-tuple-element.1331) | copy-start | bytes 1769476 | tf_op jit(solution)/shard_map/cond
  715.4 22.2 %collective-permute-start.2 = (bf16[1,512,768]{2,1,0:T(8,128)(2,1)}, bf16[1,512,768]{2,1,0:T(8,128)(2,1)}, u32[]{:S(2)}, u32[]{:S(2)}) collective-permute-start(bf16[1,512,768]{2,1,0:T(8,128)(2,1)} %get-tuple-element.1626), channel_id=1, source_target_pairs={{0,1},{2,3},{4,5},{6,7},{8,9},{10,11},{12,13},{14,15},{16,17},{18,... | collective-permute-start | bytes 2359304 | tf_op jit(solution)/shard_map/ppermute | solution.py:45
  720.1 66.9 %copy-start.150 = (f32[768]{0:T(1024)}, f32[768]{0:T(1024)S(1)}, u32[]{:S(2)}) copy-start(f32[768]{0:T(1024)S(1)} %get-tuple-element.2727) | copy-start | bytes 9220
  767.0 15.8 copy-start.32
  788.8 49.3 %copy-start.166 = (s32[512]{0:T(512)S(1)}, s32[512]{0:T(512)}, u32[]{:S(2)}) copy-start(s32[512]{0:T(512)} %sub.613) | copy-start | bytes 6148
  794.6 43.5 %copy-start.18 = (f32[512,768]{0,1:T(8,128)}, f32[512,768]{0,1:T(8,128)S(1)}, u32[]{:S(2)}) copy-start(f32[512,768]{0,1:T(8,128)S(1)} %get-tuple-element.1627) | copy-start | bytes 4718596
  838.1 121.2 %copy-start.139 = (s32[2,16,32]{2,0,1:T(2,128)S(1)}, s32[2,16,32]{2,0,1:T(2,128)}, u32[]{:S(2)}) copy-start(s32[2,16,32]{2,0,1:T(2,128)} %copy-done.138) | copy-start | bytes 12292
  955.7 10.1 collective-permute-start.3
  960.9 203.8 %all-to-all-start.2 = ((bf16[16,32,768]{2,1,0:T(8,128)(2,1)}), bf16[16,32,768]{2,1,0:T(8,128)(2,1)}, u32[]{:S(2)}, u32[]{:S(2)}) async-start(bf16[16,32,768]{2,1,0:T(8,128)(2,1)} %bitcast.628), calls=%async_computation.2 | async-start | bytes 1572864 | tf_op jit(solution)/shard_map/all_to_all | solution.py:66
  967.1 19.5 %copy-start.159 = (bf16[384]{0:T(512)(128)(2,1)S(1)}, bf16[384]{0:T(512)(128)(2,1)}, u32[]{:S(2)}) copy-start(bf16[384]{0:T(512)(128)(2,1)} %get-tuple-element.2942) | copy-start | bytes 2308
  967.1 19.5 %copy-start.163 = (bf16[384]{0:T(512)(128)(2,1)S(1)}, bf16[384]{0:T(512)(128)(2,1)}, u32[]{:S(2)}) copy-start(bf16[384]{0:T(512)(128)(2,1)} %get-tuple-element.2943) | copy-start | bytes 2308
  967.1 19.5 %copy-start.216 = (bf16[192]{0:T(256)(128)(2,1)S(1)}, bf16[192]{0:T(256)(128)(2,1)}, u32[]{:S(2)}) copy-start(bf16[192]{0:T(256)(128)(2,1)} %get-tuple-element.2944) | copy-start | bytes 1156
  986.7 52.2 %copy-start.165 = (s32[512]{0:T(512)S(1)}, s32[512]{0:T(512)}, u32[]{:S(2)}) copy-start(s32[512]{0:T(512)} %sub.617) | copy-start | bytes 6148
  992.2 46.7 %copy-start.19 = (f32[512,768]{0,1:T(8,128)}, f32[512,768]{0,1:T(8,128)S(1)}, u32[]{:S(2)}) copy-start(f32[512,768]{0,1:T(8,128)S(1)} %get-tuple-element.1654) | copy-start | bytes 4718596
  992.2 46.7 %copy-start.92 = (bf16[512,384]{0,1:T(8,128)(2,1)}, bf16[512,384]{0,1:T(8,128)(2,1)S(1)}, u32[]{:S(2)}) copy-start(bf16[512,384]{0,1:T(8,128)(2,1)S(1)} %get-tuple-element.1664) | copy-start | bytes 1179652
  1164.7 35.7 %all-to-all-start.3 = ((bf16[16,32,768]{2,1,0:T(8,128)(2,1)}), bf16[16,32,768]{2,1,0:T(8,128)(2,1)}, u32[]{:S(2)}, u32[]{:S(2)}) async-start(bf16[16,32,768]{2,1,0:T(8,128)(2,1)} %bitcast.150), calls=%async_computation.3 | async-start | bytes 1572864 | tf_op jit(solution)/shard_map/all_to_all | solution.py:66
  1191.5 194.7 %collective-permute-start.4 = (bf16[1,512,768]{2,1,0:T(8,128)(2,1)}, bf16[1,512,768]{2,1,0:T(8,128)(2,1)}, u32[]{:S(2)}, u32[]{:S(2)}) collective-permute-start(bf16[1,512,768]{2,1,0:T(8,128)(2,1)} %get-tuple-element.1651), channel_id=1, source_target_pairs={{1,0},{3,2},{5,4},{7,6},{9,8},{11,10},{13,12},{15,14},{17,16},{19,... | collective-permute-start | bytes 2359304 | tf_op jit(solution)/shard_map/ppermute | solution.py:45
  1203.7 182.6 %copy-start.151 = (f32[768]{0:T(1024)S(1)}, f32[768]{0:T(1024)}, u32[]{:S(2)}) copy-start(f32[768]{0:T(1024)} %copy-done.150) | copy-start | bytes 9220
  1203.7 182.6 %copy-start.153 = (f32[512]{0:T(512)S(1)}, f32[512]{0:T(512)}, u32[]{:S(2)}) copy-start(f32[512]{0:T(512)} %copy-done.152) | copy-start | bytes 6148
  1208.4 183.2 %copy-start.184 = (f32[384]{0:T(512)}, f32[384]{0:T(512)S(1)}, u32[]{:S(2)}) copy-start(f32[384]{0:T(512)S(1)} %get-tuple-element.1725) | copy-start | bytes 4612
  1208.4 183.2 %copy-start.185 = (f32[384]{0:T(512)}, f32[384]{0:T(512)S(1)}, u32[]{:S(2)}) copy-start(f32[384]{0:T(512)S(1)} %get-tuple-element.1729) | copy-start | bytes 4612
  1208.4 183.2 %copy-start.208 = (f32[192]{0:T(256)}, f32[192]{0:T(256)S(1)}, u32[]{:S(2)}) copy-start(f32[192]{0:T(256)S(1)} %get-tuple-element.1717) | copy-start | bytes 2308
  1208.4 183.2 %copy-start.209 = (f32[192]{0:T(256)}, f32[192]{0:T(256)S(1)}, u32[]{:S(2)}) copy-start(f32[192]{0:T(256)S(1)} %get-tuple-element.1721) | copy-start | bytes 2308
  1208.4 180.1 %copy-start.12 = (f32[512,768]{1,0:T(8,128)S(1)}, f32[512,768]{1,0:T(8,128)}, u32[]{:S(2)}) copy-start(f32[512,768]{1,0:T(8,128)} %copy-done.11) | copy-start | bytes 4718596
  1468.0 33.8 %collective-permute-start.5 = (bf16[1,512,768]{2,1,0:T(8,128)(2,1)}, bf16[1,512,768]{2,1,0:T(8,128)(2,1)}, u32[]{:S(2)}, u32[]{:S(2)}) collective-permute-start(bf16[1,512,768]{2,1,0:T(8,128)(2,1)} %convert_bitcast_fusion.1), channel_id=1, source_target_pairs={{1,0},{3,2},{5,4},{7,6},{9,8},{11,10},{13,12},{15,14},{17,16},{19,... | collective-permute-start | bytes 2359304 | tf_op jit(solution)/shard_map/ppermute | solution.py:45
  1476.2 26.9 %copy-start.111 = (f32[384,192]{0,1:T(8,128)}, f32[384,192]{0,1:T(8,128)S(1)}, u32[]{:S(2)}) copy-start(f32[384,192]{0,1:T(8,128)S(1)} %get-tuple-element.1691) | copy-start | bytes 884740
  1476.2 26.9 %copy-start.113 = (f32[192,384]{1,0:T(8,128)}, f32[192,384]{1,0:T(8,128)S(1)}, u32[]{:S(2)}) copy-start(f32[192,384]{1,0:T(8,128)S(1)} %get-tuple-element.1706) | copy-start | bytes 884740
  1476.2 26.9 %copy-start.115 = (f32[384,192]{0,1:T(8,128)}, f32[384,192]{0,1:T(8,128)S(1)}, u32[]{:S(2)}) copy-start(f32[384,192]{0,1:T(8,128)S(1)} %get-tuple-element.1702) | copy-start | bytes 884740
  1476.3 26.9 %copy-start.117 = (f32[192,384]{1,0:T(8,128)}, f32[192,384]{1,0:T(8,128)S(1)}, u32[]{:S(2)}) copy-start(f32[192,384]{1,0:T(8,128)S(1)} %get-tuple-element.1710) | copy-start | bytes 884740
  1476.3 26.9 %copy-start.186 = (f32[384]{0:T(512)}, f32[384]{0:T(512)S(1)}, u32[]{:S(2)}) copy-start(f32[384]{0:T(512)S(1)} %get-tuple-element.1726) | copy-start | bytes 4612
  1476.3 26.9 %copy-start.187 = (f32[384]{0:T(512)}, f32[384]{0:T(512)S(1)}, u32[]{:S(2)}) copy-start(f32[384]{0:T(512)S(1)} %get-tuple-element.1730) | copy-start | bytes 4612
  1476.3 26.9 %copy-start.210 = (f32[192]{0:T(256)}, f32[192]{0:T(256)S(1)}, u32[]{:S(2)}) copy-start(f32[192]{0:T(256)S(1)} %get-tuple-element.1718) | copy-start | bytes 2308
  1476.3 26.9 %copy-start.211 = (f32[192]{0:T(256)}, f32[192]{0:T(256)S(1)}, u32[]{:S(2)}) copy-start(f32[192]{0:T(256)S(1)} %get-tuple-element.1722) | copy-start | bytes 2308
  1589.1 17.4 copy-start.112
  1589.1 17.4 copy-start.116
  1615.1 28.0 %collective-permute-start.6 = (bf16[64,48,48]{0,2,1:T(8,128)(2,1)}, bf16[64,48,48]{0,2,1:T(8,128)(2,1)}, u32[]{:S(2)}, u32[]{:S(2)}) collective-permute-start(bf16[64,48,48]{0,2,1:T(8,128)(2,1)} %copy.612), channel_id=1, source_target_pairs={{0,1},{1,0},{2,3},{3,2},{4,5},{5,4},{6,7},{7,6},{8,9},{9,8},{10,11... | collective-permute-start | bytes 884744 | tf_op jit(solution)/shard_map/ppermute | solution.py:39
  1616.6 19.0 %collective-permute-start.7 = (bf16[576]{0:T(1024)(128)(2,1)S(1)}, bf16[576]{0:T(1024)(128)(2,1)S(1)}, u32[]{:S(2)}, u32[]{:S(2)}) collective-permute-start(bf16[576]{0:T(1024)(128)(2,1)S(1)} %pad_maximum_fusion.6), channel_id=1, source_target_pairs={{0,1},{1,0},{2,3},{3,2},{4,5},{5,4},{6,7},{7,6},{8,9},{9,8},{10,11... | collective-permute-start | bytes 3464 | tf_op jit(solution)/shard_map/ppermute | solution.py:39
  1636.3 23.8 %all-to-all-start.5 = ((bf16[16,1,108]{2,1,0:T(2,128)(2,1)}), bf16[16,1,108]{2,1,0:T(2,128)(2,1)S(1)}, u32[]{:S(2)}, u32[]{:S(2)}) async-start(bf16[16,1,108]{2,1,0:T(2,128)(2,1)} %convert_element_type.724), calls=%async_computation.5 | async-start | bytes 16384 | tf_op jit(solution)/shard_map/all_to_all | solution.py:66
  1660.1 38.4 %all-to-all-start.4 = ((bf16[16,2,23040]{2,1,0:T(2,128)(2,1)}), bf16[16,2,23040]{2,1,0:T(2,128)(2,1)S(1)}, u32[]{:S(2)}, u32[]{:S(2)}) async-start(bf16[16,2,23040]{2,1,0:T(2,128)(2,1)} %reshape.1511), calls=%async_computation.4 | async-start | bytes 2949120 | tf_op jit(solution)/shard_map/all_to_all | solution.py:66
  1667.7 83.8 %copy-start.82 = (f32[1,20,48,48]{3,2,1,0:T(8,128)S(1)}, f32[1,20,48,48]{3,2,1,0:T(8,128)}, u32[]{:S(2)}) copy-start(f32[1,20,48,48]{3,2,1,0:T(8,128)} %param.74) | copy-start | bytes 552964
  1703.4 49.2 %copy-start.129 = (f32[1,20,48,48]{3,2,1,0:T(8,128)S(1)}, f32[1,20,48,48]{3,2,1,0:T(8,128)}, u32[]{:S(2)}) copy-start(f32[1,20,48,48]{3,2,1,0:T(8,128)} %param.75) | copy-start | bytes 552964
  1703.4 50.9 %copy-start.130 = (f32[1,20,48,48]{3,2,1,0:T(8,128)S(1)}, f32[1,20,48,48]{3,2,1,0:T(8,128)}, u32[]{:S(2)}) copy-start(f32[1,20,48,48]{3,2,1,0:T(8,128)} %param.76) | copy-start | bytes 552964
  1706.5 50.2 %copy-start.84 = (f32[1,20,48,48]{3,2,1,0:T(8,128)S(1)}, f32[1,20,48,48]{3,2,1,0:T(8,128)}, u32[]{:S(2)}) copy-start(f32[1,20,48,48]{3,2,1,0:T(8,128)} %param.73) | copy-start | bytes 552964
  1706.5 50.2 %copy-start.131 = (f32[1,20,48,48]{3,2,1,0:T(8,128)S(1)}, f32[1,20,48,48]{3,2,1,0:T(8,128)}, u32[]{:S(2)}) copy-start(f32[1,20,48,48]{3,2,1,0:T(8,128)} %param.78) | copy-start | bytes 552964
  (154 other events, 766.7 us)
Sparse Core Ops, SparseCore 0:
  35.1 253.4 all-gather.18
where the time goes:
time: 1780 us; the launch traced here: 1770 us
  blocking collectives  738 us (41%)
  local copies, waits for them, and re-layouts  294 us (17%)
  matrix products  259 us (15%)
  waiting for transfers between devices  228 us (13%)
  other arithmetic  110 us (6%)
  starting transfers between devices  94.5 us (5%)
  between operations  23 us (1%)
  loops' own time  18.7 us (1%)
    all_gather x1, blocking collectives, shards(): lax.all_gather(token_ids, 'dp', axis=1, tiled=True)  265 us
    all_gather x6, blocking collectives, joined_2(): everything = jax.tree.map(lambda part: lax.all_gather(part, axis), value)  219 us
    ppermute x4, waiting for transfers between devices, from_behind(): lax.ppermute(value, axis, [(source, source + steps) for source in range(f...  198 us
    dot_general x16, matrix products, matmul_t(): lax.dot_general(left, right, (((left.ndim - 1,), (1,)), ((), ())), prefer...  90.3 us
    all_gather x2, blocking collectives, shards(): lax.all_gather(chosen.astype(jnp.bfloat16), 'dp', axis=0, tiled=True)  87.2 us
    dot_general x20, matrix products, matmul(): return jnp.dot(left, right, preferred_element_type=jnp.float32)  86.1 us
    gather x2, local copies, waits for them, and re-layouts, shards(): picked = jnp.take(columns, ordered, axis=0)  72.2 us
    another operation x62, local copies, waits for them, and re-layouts  60 us
  transfers between devices with their start and end apart: 15, of which 3 were waited for; matrix products, arithmetic and copies ran while one was open for 15% of the time, Pallas kernels for 0%

commit v1 on v0

v1 whole, which is shorter than its diff:
```python
import jax
import jax.numpy as jnp
import numpy as np
from jax import lax
from jax.sharding import PartitionSpec as P

D = 768
HEADS = 12
HEAD_DIM = 64
BOT = 384
INV_H = 192
SEQ = 512
COUNT = 32
MICRO = 2
BLOCK = 48
STEP = 10
HALF = 384
IDS = SEQ + COUNT

HIGHEST = lax.Precision.HIGHEST
NORM_EPS = 1e-12
CLIP_NORM = 0.02
FIRST_DECAY = 0.9
STAT_DECAY = 0.99
MAT_RATE = 0.1
MAT_DECAY = 0.01
VEC_RATE = 0.05
VEC_SECOND = 0.999
VEC_EPS = 1e-08
VEC_DECAY = 0.01
F32 = jnp.float32
BF16 = jnp.bfloat16

CDF_SCALE = 0.42 / 2.0**0.5
CDF_POLY = (
    0.2368242366796694,
    0.239585811361218,
    0.1947261443420679,
    0.2687426685879861,
    -0.13052645834187002,
    0.4406726942003943,
    -0.32025628294963193,
    0.07023101752398136,
)


def matmul(left, right):
    return jnp.dot(left, right, preferred_element_type=F32)


def matmul_t(left, right):
    return lax.dot_general(left, right, (((1,), (1,)), ((), ())), preferred_element_type=F32)


def inner_rows(left, right):
    return lax.dot_general(left, right, (((0,), (0,)), ((), ())), preferred_element_type=F32)


def low(values):
    return values.astype(BF16)


def gelu_both(values):
    ratio = 1.0 / (1.0 + CDF_SCALE * jnp.abs(values))
    poly = jnp.full_like(ratio, 0.5 * CDF_POLY[-1])
    for factor in CDF_POLY[-2::-1]:
        poly = poly * ratio + 0.5 * factor
    bell = jnp.exp(-0.5 * values * values)
    tail = bell * (poly * ratio)
    cdf = jnp.where(values < 0, tail, 1.0 - tail)
    return values * cdf, cdf + values * (bell * (2.0 * np.pi) ** -0.5)


def layer_norm(values, gain, shift):
    centered = values - jnp.mean(values, -1, keepdims=True)
    inverse = lax.rsqrt(jnp.mean(centered * centered, -1, keepdims=True) + NORM_EPS)
    normal = centered * inverse
    return normal * gain + shift, (normal, inverse)


def norm_back(incoming, kept, gain):
    normal, inverse = kept
    scaled = incoming * gain
    return inverse * (
        scaled
        - jnp.mean(scaled, -1, keepdims=True)
        - normal * jnp.mean(scaled * normal, -1, keepdims=True)
    )


def to_blocks(matrix):
    rows_in, cols_in = matrix.shape
    return (
        matrix.reshape(rows_in // BLOCK, BLOCK, cols_in // BLOCK, BLOCK)
        .transpose(0, 2, 1, 3)
        .reshape(-1, BLOCK, BLOCK)
    )


def from_blocks(blocks, rows_in, cols_in):
    return (
        blocks.reshape(rows_in // BLOCK, cols_in // BLOCK, BLOCK, BLOCK)
        .transpose(0, 2, 1, 3)
        .reshape(rows_in, cols_in)
    )


def split_params(blocks, vector):
    adapter_count = D * BOT // BLOCK**2
    half_count = HALF * INV_H // BLOCK**2
    split_at = 2 * adapter_count
    adapter = (
        from_blocks(blocks[:adapter_count], D, BOT),
        vector[:BOT],
        from_blocks(blocks[adapter_count:split_at], BOT, D),
        vector[BOT : BOT + D],
    )
    coupling = (
        from_blocks(blocks[split_at : split_at + half_count], HALF, INV_H),
        vector[BOT + D : BOT + D + INV_H],
        from_blocks(blocks[split_at + half_count :], INV_H, HALF),
        vector[BOT + D + INV_H :],
    )
    return adapter, coupling


def join_params(adapter, coupling):
    blocks = jnp.concatenate(
        [to_blocks(adapter[0]), to_blocks(adapter[2]), to_blocks(coupling[0]), to_blocks(coupling[2])]
    )
    return blocks, jnp.concatenate([adapter[1], adapter[3], coupling[1], coupling[3]])


def branch_fwd(values, params):
    w_down, b_down, w_up, b_up = params
    low_in = low(values)
    active, slope = gelu_both(matmul(low_in, w_down) + b_down.astype(F32))
    active = low(active)
    return matmul(active, w_up) + b_up.astype(F32), (low_in, active, slope)


def branch_back(incoming, kept, params, inward=True):
    w_down, b_down, w_up, b_up = params
    low_in, active, slope = kept
    grad_low = low(incoming)
    hidden_grad = low(matmul_t(grad_low, w_up) * slope)
    weight_grads = (
        inner_rows(low_in, hidden_grad),
        jnp.sum(hidden_grad.astype(F32), 0),
        inner_rows(active, grad_low),
        jnp.sum(grad_low.astype(F32), 0),
    )
    return matmul_t(hidden_grad, w_down) if inward else None, weight_grads


def heads_of(rows):
    return rows.reshape(rows.shape[0], -1, HEAD_DIM)


def attend_fwd(query, key, value, length):
    scores = jnp.einsum("qhd,khd->hqk", heads_of(query), heads_of(key), preferred_element_type=F32)
    scores = scores * HEAD_DIM**-0.5
    scores = jnp.where((jnp.arange(SEQ) < length)[None, None, :], scores, -1e30)
    exponent = jnp.exp(scores - jnp.max(scores, -1, keepdims=True))
    soft = exponent * (1.0 / jnp.sum(exponent, -1, keepdims=True))
    mixed = jnp.einsum("hqk,khd->qhd", low(soft), heads_of(value), preferred_element_type=F32)
    return low(mixed.reshape(query.shape)), soft


def attend_back(query, key, value, soft, mixed_grad):
    grad_heads = heads_of(mixed_grad)
    weight_grad = jnp.einsum("qhd,khd->hqk", grad_heads, heads_of(value), preferred_element_type=F32)
    score_grad = low(soft * (weight_grad - jnp.sum(weight_grad * soft, -1, keepdims=True)))
    scale = HEAD_DIM**-0.5
    query_grad = jnp.einsum("hqk,khd->qhd", score_grad, heads_of(key), preferred_element_type=F32) * scale
    key_grad = jnp.einsum("hqk,qhd->khd", score_grad, heads_of(query), preferred_element_type=F32) * scale
    value_grad = jnp.einsum("hqk,qhd->khd", low(soft), grad_heads, preferred_element_type=F32)
    return tuple(low(grad.reshape(-1, D)) for grad in (query_grad, key_grad, value_grad))


def rest_fwd(hidden, mixed, weights):
    w_out, w_up, w_down, gains, adapter = weights
    attended, kept_one = layer_norm(hidden + matmul(mixed, w_out), gains[0], gains[1])
    active, slope = gelu_both(matmul(low(attended), w_up))
    summed = matmul(low(active), w_down) + attended
    branch_out, kept_branch = branch_fwd(summed, adapter)
    result, kept_two = layer_norm(summed + branch_out, gains[2], gains[3])
    return result, (kept_one, low(slope), kept_branch, kept_two)


def rest_back(incoming, kept, weights):
    w_out, w_up, w_down, gains, adapter = weights
    kept_one, slope, kept_branch, kept_two = kept
    second_grad = norm_back(incoming, kept_two, gains[2])
    branch_grad, adapter_grads = branch_back(second_grad, kept_branch, adapter)
    summed_grad = second_grad + branch_grad
    inner_grad = low(matmul_t(low(summed_grad), w_down) * slope.astype(F32))
    attended_grad = summed_grad + matmul_t(inner_grad, w_up)
    start_grad = norm_back(attended_grad, kept_one, gains[0])
    return start_grad, low(matmul_t(low(start_grad), w_out)), adapter_grads


def swap_add(own, other):
    came = lax.ppermute(low(other), "section", [(0, 1), (1, 0)])
    return own + came.astype(F32)


def pick(first_section, both):
    return jnp.where(first_section, both[0], both[1])


def plan_requests(ids, vocab_rows, slots):
    earlier = jnp.arange(IDS)[None, :] < jnp.arange(IDS)[:, None]
    same_id = ids[:, :, None] == ids[:, None, :]
    first = jnp.logical_not(jnp.any(same_id & earlier, -1))
    owner = ids // vocab_rows
    same_owner = owner[:, :, None] == owner[:, None, :]
    rank = jnp.sum((same_owner & earlier & first[:, None, :]).astype(jnp.int32), -1)
    slot = jnp.sum(jnp.where(same_id & first[:, None, :], rank[:, None, :], 0), -1)
    rounds = jnp.max(rank) // slots + 1
    return owner, slot, first, rounds


def fetch_rows(table, ids, first_section, weight_part, slots):
    parts = lax.axis_size("dp")
    vocab_rows = table.shape[0]
    owner, slot, first, rounds = plan_requests(ids, vocab_rows, slots)
    ids, owner, slot, first = (pick(first_section, both) for both in (ids, owner, slot, first))
    local = ids - owner * vocab_rows

    def places(turn):
        here = slot - turn * slots
        spot = jnp.where((here >= 0) & (here < slots), owner * slots + here, -1)
        return spot[:, None] == jnp.arange(parts * slots)[None, :]

    def wanted(hits):
        return jnp.sum(jnp.where(hits & first[:, None], local[:, None], 0), 0).reshape(parts, slots)

    def answer(asked, hits):
        rows = table.at[asked.reshape(-1)].get(mode="promise_in_bounds").reshape(parts, slots, D)
        came = lax.all_to_all(rows, "dp", 0, 0).reshape(parts * slots, D)
        return matmul(hits.astype(BF16), came)

    hits = places(0)
    extra = jnp.broadcast_to(jnp.stack([rounds, weight_part])[None], (parts, 2))
    asked = lax.all_to_all(jnp.concatenate([wanted(hits), extra], 1), "dp", 0, 0)
    total_rounds = jnp.max(asked[:, slots])
    weight_sum = jnp.sum(asked[:, slots + 1])
    rows = answer(asked[:, :slots], hits)

    def more(state):
        return state[0] < total_rounds

    def another(state):
        turn, rows = state
        hits = places(turn)
        asked = lax.all_to_all(wanted(hits), "dp", 0, 0)
        return turn + 1, rows + answer(asked, hits)

    return lax.while_loop(more, another, (jnp.int32(1), rows))[1], weight_sum.astype(F32)


def three_low(values):
    high = low(values)
    rest = values - high.astype(F32)
    middle = low(rest)
    return [high, middle, low(rest - middle.astype(F32))]


def head_parts(rows, table):
    logits = matmul_t(rows, table)
    highest = jnp.max(logits, -1, keepdims=True)
    exponent = jnp.exp(logits - highest)
    return matmul(low(exponent), table), highest, jnp.sum(exponent, -1, keepdims=True)


def head(normed, target_rows, row_weights, weight_sum, table):
    parts = lax.axis_size("dp")
    mine = low(normed)
    rows = lax.all_to_all(
        jnp.broadcast_to(mine[None], (parts, COUNT, D)), "dp", 0, 0
    ).reshape(parts * COUNT, D)
    mixed, highest, exp_total = head_parts(rows, table)
    stats = jnp.concatenate(three_low(highest) + three_low(exp_total), -1)
    stats = jnp.pad(stats, ((0, 0), (0, 128 - stats.shape[1])))
    packed = jnp.concatenate([low(mixed), stats], -1).reshape(parts, COUNT, D + 128)
    came = lax.all_to_all(packed, "dp", 0, 0).astype(F32)
    highest = jnp.sum(came[:, :, D : D + 3], -1)
    exp_total = jnp.sum(came[:, :, D + 3 : D + 6], -1)
    top = jnp.max(highest, 0)
    factor = jnp.exp(highest - top)
    total = jnp.sum(exp_total * factor, 0)
    target_logit = jnp.sum(mine.astype(F32) * target_rows, -1)
    loss = jnp.sum(row_weights * (top + jnp.log(total) - target_logit))
    expected = jnp.sum(came[:, :, :D] * (factor / total)[:, :, None], 0)
    return loss, (row_weights / weight_sum)[:, None] * (expected - target_rows)


def shards(
    token_ids,
    lengths,
    positions,
    targets,
    loss_weights,
    embed_table,
    pos_table,
    norm_params,
    base_qkv,
    base_out,
    base_up,
    base_down,
    master,
    momentum,
    stat_left,
    stat_right,
    root_left,
    root_right,
    vectors,
    vec_first,
    vec_second,
):
    parts = lax.axis_size("dp")
    first_section = lax.axis_index("section") == 0
    slots = -(-IDS * 5 // (4 * parts * 16)) * 16

    ids = jnp.concatenate([token_ids[:, 0], targets[:, 0]], -1)
    weight_part = jnp.sum(loss_weights)
    fetched, weight_sum = fetch_rows(embed_table, ids, first_section, weight_part, slots)
    length = pick(first_section, lengths[:, 0])
    spots = pick(first_section, positions[:, 0])
    row_weights = pick(first_section, loss_weights[:, 0]).astype(F32)

    own_blocks = master.shape[1]
    own_vector = vectors.shape[1]
    flat = low(jnp.concatenate([master[0].reshape(-1), vectors[0]]))
    gathered = lax.all_gather(flat, ("section", "dp")).reshape(MICRO, parts, -1)
    all_blocks = gathered[:, :, : own_blocks * BLOCK**2].reshape(MICRO, parts * own_blocks, BLOCK, BLOCK)
    all_vectors = gathered[:, :, own_blocks * BLOCK**2 :].reshape(MICRO, parts * own_vector)
    params = [split_params(all_blocks[s], all_vectors[s]) for s in range(MICRO)]
    adapters = [pair[0] for pair in params]
    coupling_one, coupling_two = (pair[1] for pair in params)
    norms = lax.all_gather(norm_params, "section", axis=0, tiled=True)
    w_qkv, w_out, w_up, w_down = (
        lax.all_gather(weight, "section", axis=0, tiled=True)
        for weight in (base_qkv, base_out, base_up, base_down)
    )
    rests = [(w_out[s], w_up[s], w_down[s], norms[s, 2:], adapters[s]) for s in range(MICRO)]

    started, _ = layer_norm(fetched[:SEQ] + pos_table.astype(F32), norms[0, 0], norms[0, 1])
    one_out, kept_one = branch_fwd(started[:, HALF:], coupling_one)
    left_half = started[:, :HALF] + one_out
    two_out, kept_two = branch_fwd(left_half, coupling_two)
    hidden = jnp.concatenate([left_half, started[:, HALF:] + two_out], -1)
    projected = low(matmul(low(hidden), w_qkv[0]))
    query, key, value = projected[:, :D], projected[:, D : 2 * D], projected[:, 2 * D :]
    mixed, soft = attend_fwd(query, key, value, length)
    section_out, kept_rest = rest_fwd(hidden, mixed, rests[0])
    section_out = low(section_out)

    chosen = (spots[:, None] == jnp.arange(SEQ)[None, :]).astype(BF16)
    at_spots = matmul(chosen, section_out)
    query_1 = low(matmul(low(at_spots), w_qkv[1][:, :D]))
    key_value = low(matmul(section_out, w_qkv[1][:, D:]))
    key_1, value_1 = key_value[:, :D], key_value[:, D:]
    mixed_1, soft_1 = attend_fwd(query_1, key_1, value_1, length)
    out_1, kept_rest_1 = rest_fwd(at_spots, mixed_1, rests[1])
    two_last, kept_two_last = branch_fwd(out_1[:, :HALF], coupling_two)
    right_last = out_1[:, HALF:] - two_last
    one_last, kept_one_last = branch_fwd(right_last, coupling_one)
    normed, kept_head = layer_norm(
        jnp.concatenate([out_1[:, :HALF] - one_last, right_last], -1), norms[1, 0], norms[1, 1]
    )

    loss_part, normed_grad = head(normed, fetched[SEQ:], row_weights, weight_sum, embed_table)

    restored_grad = norm_back(normed_grad, kept_head, norms[1, 0])
    left_grad = restored_grad[:, :HALF]
    into_right, grads_one = branch_back(-left_grad, kept_one_last, coupling_one)
    right_grad = restored_grad[:, HALF:] + into_right
    into_left, grads_two = branch_back(-right_grad, kept_two_last, coupling_two)
    out_grad = jnp.concatenate([left_grad + into_left, right_grad], -1)
    start_grad, mixed_grad, adapter_grads_1 = rest_back(out_grad, kept_rest_1, rests[1])
    query_grad, key_grad, value_grad = attend_back(query_1, key_1, value_1, soft_1, mixed_grad)
    spot_grad = start_grad + matmul_t(query_grad, w_qkv[1][:, :D])
    section_grad = (
        lax.dot_general(chosen.astype(F32), spot_grad, (((0,), (0,)), ((), ())), precision=HIGHEST)
        + matmul_t(key_grad, w_qkv[1][:, D : 2 * D])
        + matmul_t(value_grad, w_qkv[1][:, 2 * D :])
    )
    section_grad = low(section_grad).astype(F32)

    start_grad, mixed_grad, adapter_grads_0 = rest_back(section_grad, kept_rest, rests[0])
    query_grad, key_grad, value_grad = attend_back(query, key, value, soft, mixed_grad)
    hidden_grad = start_grad + matmul_t(
        jnp.concatenate([query_grad, key_grad, value_grad], -1), w_qkv[0]
    )
    into_left, first_two = branch_back(hidden_grad[:, HALF:], kept_two, coupling_two)
    _, first_one = branch_back(hidden_grad[:, :HALF] + into_left, kept_one, coupling_one, False)
    grads_one = jax.tree.map(jnp.add, grads_one, first_one)
    grads_two = jax.tree.map(jnp.add, grads_two, first_two)

    joined = [join_params(adapter_grads_0, grads_one), join_params(adapter_grads_1, grads_two)]
    flat = [
        jnp.concatenate(
            [blocks.reshape(parts, own_blocks * BLOCK**2), vector.reshape(parts, own_vector)], 1
        )
        for blocks, vector in joined
    ]
    summed = swap_add(
        jnp.where(first_section, flat[0], flat[1]), jnp.where(first_section, flat[1], flat[0])
    )
    owned = jnp.sum(lax.all_to_all(low(summed), "dp", 0, 0).astype(F32), 0)
    grad_blocks = owned[: own_blocks * BLOCK**2].reshape(own_blocks, BLOCK, BLOCK)
    grad_vector = owned[own_blocks * BLOCK**2 :]

    squares = jnp.sum(owned * owned)
    pair = jnp.broadcast_to(jnp.stack([squares, loss_part])[None], (parts * MICRO, 2))
    totals = jnp.sum(lax.all_to_all(pair, ("dp", "section"), 0, 0), 0)
    grad_norm = jnp.sqrt(totals[0])
    loss_sum = totals[1]
    factor = CLIP_NORM / jnp.maximum(grad_norm, CLIP_NORM)
    clipped = grad_blocks * factor
    clipped_vector = grad_vector * factor
    momentum_new = FIRST_DECAY * momentum[0] + (1.0 - FIRST_DECAY) * clipped
    left_new = STAT_DECAY * stat_left[0] + (1.0 - STAT_DECAY) * jnp.einsum(
        "nij,nkj->nik", clipped, clipped, precision=HIGHEST
    )
    right_new = STAT_DECAY * stat_right[0] + (1.0 - STAT_DECAY) * jnp.einsum(
        "nji,njk->nik", clipped, clipped, precision=HIGHEST
    )
    direction = jnp.einsum("nij,njk->nik", root_left[0], momentum_new, precision=HIGHEST)
    direction = jnp.einsum("nij,njk->nik", direction, root_right[0], precision=HIGHEST)
    master_new = master[0] - MAT_RATE * (direction + MAT_DECAY * master[0])
    first_new = FIRST_DECAY * vec_first[0] + (1.0 - FIRST_DECAY) * clipped_vector
    second_new = VEC_SECOND * vec_second[0] + (1.0 - VEC_SECOND) * clipped_vector * clipped_vector
    corrected_first = first_new / (1.0 - FIRST_DECAY**STEP)
    corrected_second = second_new / (1.0 - VEC_SECOND**STEP)
    vectors_new = vectors[0] - VEC_RATE * (
        corrected_first / (jnp.sqrt(corrected_second) + VEC_EPS) + VEC_DECAY * vectors[0]
    )
    return (
        clipped[None],
        momentum_new[None],
        left_new[None],
        right_new[None],
        master_new[None],
        master_new.astype(BF16)[None],
        first_new[None],
        second_new[None],
        vectors_new[None],
        grad_norm,
        loss_sum,
        weight_sum,
    )


def solution(mesh):
    rows = P(None, "dp", None)
    section = P("section", None, None)
    blocks = P("section", "dp", None, None)
    biases = P("section", "dp")
    return jax.shard_map(
        shards,
        mesh=mesh,
        in_specs=(rows, P(None, "dp"), rows, rows, rows, P("dp", None), P())
        + (section,) * 5
        + (blocks,) * 6
        + (biases,) * 3,
        out_specs=(blocks,) * 6 + (biases,) * 3 + (P(),) * 3,
        check_vma=False,
    )
```

time: 1780 us -> 653 us (0.37)
  blocking collectives: 738 us -> 103 us
  waiting for transfers between devices: 228 us -> 54.8 us
  local copies, waits for them, and re-layouts: 294 us -> 184 us
  starting transfers between devices: 94.5 us -> 8.67 us
  matrix products: 259 us -> 189 us
  other arithmetic: 110 us -> 73.6 us
    all_gather x11 -> x1, blocking collectives: 645 us -> 1.84 us  [shards(): norms = lax.all_gather(norm_params, 'section', axis=0, tiled=True)]
    ppermute x8 -> x1, waiting for transfers between devices: 198 us -> 3.26 us  [swap_add(): came = lax.ppermute(low(other), 'section', [(0, 1), (1, 0)])]
    all_to_all x0 -> x4, blocking collectives: none -> 101 us  [the longest x1 41.5 us: shards(): owned = jnp.sum(lax.all_to_all(low(summed), 'dp', 0, 0).astype(F32), 0)]
    all_to_all x6 -> x2, starting transfers between devices: 86.9 us -> 8.41 us  [the longest x1 4.71 us: head(): came = lax.all_to_all(packed, 'dp', 0, 0).astype(F32)]
    dot_general x50 -> x56, matrix products: 238 us -> 161 us  [the longest x20 64.8 us: matmul_t(): lax.dot_general(left, right, (((1,), (1,)), ((), ())), preferred_element_...]
    gather x4 -> x1, local copies, waits for them, and re-layouts: 75.2 us -> 9.74 us  [answer(): table.at[asked.reshape(-1)].get(mode='promise_in_bounds')]
    another operation x62 -> x0, local copies, waits for them, and re-layouts: 60 us -> none
    unnamed x1 -> x0, blocking collectives: 51.5 us -> none
  transfers between devices with their start and end apart: 15 -> 8, of which waited for: 3 -> 3; matrix products, arithmetic and copies ran while one was open for 15% -> 19% of each run, Pallas kernels for 0% -> 0%
where the time goes in v1:
time: 653 us; the launch traced here: 650 us
  matrix products  189 us (29%)
  local copies, waits for them, and re-layouts  184 us (28%)
  blocking collectives  103 us (16%)
  other arithmetic  73.6 us (11%)
  waiting for transfers between devices  54.8 us (8%)
  between operations  23.2 us (4%)
  loops' own time  12.6 us (2%)
  starting transfers between devices  8.67 us (1%)
    dot_general x20, matrix products, matmul_t(): lax.dot_general(left, right, (((1,), (1,)), ((), ())), preferred_element_...  64.8 us
    dot_general x24, matrix products, matmul(): return jnp.dot(left, right, preferred_element_type=F32)  59.5 us
    all_to_all x1, blocking collectives, shards(): owned = jnp.sum(lax.all_to_all(low(summed), 'dp', 0, 0).astype(F32), 0)  41.5 us
    reshape x16, local copies, waits for them, and re-layouts, to_blocks(): matrix.reshape(rows_in // BLOCK, BLOCK, cols_in // BLOCK, BLOCK)  39.6 us
    all_to_all x1, blocking collectives, head(): lax.all_to_all(jnp.broadcast_to(mine[None], (parts, COUNT, D)), 'dp', 0, 0)  34.6 us
    unnamed x354, local copies, waits for them, and re-layouts  33.9 us
    all_to_all x1, waiting for transfers between devices, answer(): came = lax.all_to_all(rows, 'dp', 0, 0).reshape(parts * slots, D)  29.6 us
    reshape x2, local copies, waits for them, and re-layouts, shards(): blocks.reshape(parts, own_blocks * BLOCK ** 2)  20.5 us
  transfers between devices with their start and end apart: 8, of which 3 were waited for; matrix products, arithmetic and copies ran while one was open for 19% of the time, Pallas kernels for 0%

profile of v1, /device:TPU:0, one launch (start us, length us, event | category | flops | bytes accessed | tf_op | source)
XLA Modules:
  0.0 649.9 jit_solution(6333144552044641754)
XLA Ops:
  20.0 15.4 %all_to_all.59 = s32[16,1,50]{2,1,0:T(1,128)S(1)} all-to-all(s32[16,1,50]{2,1,0:T(1,128)S(1)} %bitcast.394), channel_id=1, replica_groups=mesh['dp'=16,'section'=2] {'dp'}, dimensions={0} | all-to-all | bytes 6400 | tf_op jit(solution)/shard_map/all_to_all | solution.py:246
  35.5 9.7 %gather_fusion.1 = bf16[768,768]{1,0:T(8,128)(2,1)} fusion(bf16[7472,768]{1,0:T(8,128)(2,1)} %param.28, s32[1024]{0:T(1024)S(1)} %pad_clamp_fusion.1), kind=kCustom, calls=%fused_computation.1 | custom fusion | bytes 2362368 | tf_op jit(solution)/shard_map/gather | solution.py:240
  45.3 3.7 all-to-all-start.3
  55.6 29.6 %all-to-all-done.3 = bf16[16,48,768]{2,1,0:T(8,128)(2,1)S(1)} async-done(((bf16[16,48,768]{2,1,0:T(8,128)(2,1)}), bf16[16,48,768]{2,1,0:T(8,128)(2,1)S(1)}, u32[]{:S(2)}, u32[]{:S(2)}) %all-to-all-start.3) | async-done | bytes 1179680 | tf_op jit(solution)/shard_map/all_to_all | solution.py:241
  87.3 12.6 %while.10 = (s32[]{:T(128)}, f32[544,768]{1,0:T(8,128)}, s32[]{:T(128)}, s32[544]{0:T(1024)S(1)}, s32[544]{0:T(1024)S(1)}, /*index=5*/pred[544]{0:T(1024)(128)(4...) while((s32[]{:T(128)}, f32[544,768]{1,0:T(8,128)}, ...), condition=%wide.region_9.10_spmd, body=%wide.region_7.9_spmd.sunk | while | flops 644241664 | bytes 10478025 | solution.py:260
  103.8 4.0 copy.294
  109.6 6.4 squeeze.44
  124.2 6.4 squeeze.46
  134.1 3.6 fusion.283
  141.3 2.3 reshape.932
  143.6 4.1 fusion.282
  150.0 3.1 copy.315
  153.0 3.8 reshape.939
  163.4 5.1 convolution_convert_fusion
  172.8 10.7 %fusion.292 = (f32[12,512]{1,0:T(8,128)S(1)}, f32[12,512,512]{1,2,0:T(8,128)}) fusion(pred[512]{0:T(512)(128)(4,1)S(1)} %iota_compare_fusion.11, bf16[512,12,64]{0,2,1:T(8,128)(2,1)} %bitcast.368, bf16[512,12,64]{0,2,1:T(8,128)(2,1)S(1)} %bitcast.354), kind=kOutput, calls=%fused_computation.589 | convolution fusion | flops 415236608 | bytes 14180864 | tf_op jit(solution)/shard_map/sub | solution.py:164
  183.5 6.7 %fusion.74 = bf16[12,64,512]{2,1,0:T(8,128)(2,1)} fusion(bf16[512,12,64]{0,2,1:T(8,128)(2,1)S(1)} %bitcast.346, f32[12,512,512]{1,2,0:T(8,128)} %get-tuple-element.144, f32[12,512]{1,0:T(8,128)S(1)} %broadcast_divide_fusion), kind=kOutput, calls=%fused_computation.143 | convolution fusion | flops 409337856 | bytes 14180352 | tf_op jit(solution)/shard_map/hqk,khd->qhd/dot_general | solution.py:166
  190.2 2.6 fusion.293
  194.2 4.1 slice_bitcast_fusion.12
  198.3 8.0 %fusion.18 = f32[512,3072]{1,0:T(8,128)} fusion(bf16[2,768,3072]{2,1,0:T(8,128)(2,1)} %all-gather.11.cloned.1.call-done, f32[512,768]{0,1:T(8,128)S(1)} %copy-done.12, f32[768]{0:T(1024)S(1)} %get-tuple-element.76, f32[768]{0:T(1024)S(1)} %get-tuple-element.77, f32[512]{0:T(512)S(1)} %add_rsqrt_fusion.1, f32[512]{0:T(512)S(1)} %broadcast_multiply_fusion.5), kind=kOutput, calls=%fused_computation.48 | convolution fusion | flops 2417885184 | bytes 12593152 | tf_op jit(solution)/shard_map/dot_general | solution.py:48
  206.3 10.5 %fusion.66 = f32[512,768]{0,1:T(8,128)S(1)} fusion(bf16[2,3072,768]{2,1,0:T(8,128)(2,1)} %all-gather.13.cloned.1.call-done, f32[512,3072]{1,0:T(8,128)} %fusion.18, f32[512,768]{0,1:T(8,128)S(1)} %copy-done.12, f32[768]{0:T(1024)S(1)} %get-tuple-element.76, f32[768]{0:T(1024)S(1)} %get-tuple-element.77, f32[512]{0:T(512)S(1)} %add_rsqrt_fusion.1, ...), kind=kOutput, calls=%fused_computation.138 | convolution fusion | flops 2460352512 | bytes 14166016 | tf_op jit(solution)/shard_map/dot_general | solution.py:48
  224.3 2.4 copy.242
  228.2 2.2 convolution_convert_fusion.6
  235.4 2.3 copy.241
  237.8 3.0 fusion.99
  246.0 3.3 fusion.21
  249.4 3.6 fusion.101
  257.8 34.6 %all_to_all.60 = bf16[16,32,768]{2,1,0:T(8,128)(2,1)S(1)} all-to-all(bf16[16,32,768]{2,1,0:T(8,128)(2,1)S(1)} %broadcast_in_dim.115), channel_id=1, replica_groups=mesh['dp'=16,'section'=2] {'dp'}, dimensions={0} | all-to-all | bytes 1572864 | tf_op jit(solution)/shard_map/all_to_all | solution.py:280
  292.4 14.0 %fusion.300 = (f32[512]{0:T(512)S(1)}, f32[512,7472]{0,1:T(8,128)}) fusion(bf16[512,768]{1,0:T(8,128)(2,1)S(1)} %bitcast.388, bf16[7472,768]{1,0:T(8,128)(2,1)} %get-tuple-element.274), kind=kOutput, calls=%fused_computation.597 | convolution fusion | flops 5880045056 | bytes 27568128 | tf_op jit(solution)/shard_map/dot_general | solution.py:52
  306.4 10.7 %fusion.70 = bf16[512,768]{1,0:T(8,128)(2,1)} fusion(bf16[7472,768]{1,0:T(8,128)(2,1)S(1)} %bitcast.336, f32[512,7472]{0,1:T(8,128)} %get-tuple-element.160, f32[512]{0:T(512)S(1)} %get-tuple-element.159), kind=kOutput, calls=%fused_computation.140 | convolution fusion | flops 5884264448 | bytes 27568128 | tf_op jit(solution)/shard_map/dot_general | solution.py:48
  317.1 7.4 %fusion.7 = f32[512]{0:T(512)S(1)} fusion(f32[512,7472]{0,1:T(8,128)} %get-tuple-element.160, f32[512]{0:T(512)S(1)} %get-tuple-element.159), kind=kLoop, calls=%fused_computation.15 | loop fusion | flops 7650816 | bytes 15306752 | tf_op jit(solution)/shard_map/reduce_sum | solution.py:274
  328.4 2.2 fusion.111
  330.6 4.7 all-to-all-start.5
  335.9 19.5 %all-to-all-done.5 = bf16[16,32,896]{2,1,0:T(8,128)(2,1)} async-done(((bf16[16,32,896]{2,1,0:T(8,128)(2,1)}), bf16[16,32,896]{2,1,0:T(8,128)(2,1)}, u32[]{:S(2)}, u32[]{:S(2)}) %all-to-all-start.5) | async-done | bytes 917536 | tf_op jit(solution)/shard_map/all_to_all | solution.py:287
  371.8 7.9 %fusion.278 = (f32[32]{0:T(128)}, f32[32]{0:T(128)}, f32[32,768]{1,0:T(8,128)}) fusion(f32[32]{0:T(128)} %copy-done.146, f32[32,768]{1,0:T(8,128)} %copy-done.40, f32[32]{0:T(128)S(1)} %copy-done.132, f32[768]{0:T(1024)S(1)} %copy-done.124, f32[32,768]{1,0:T(8,128)} %convolution_add_fusion.15, bf16[2,768,3072]{2,1,0:T(8,128)(2,1)} %all-gather.11.cloned.1.call-done, ...), kind=kOutput, calls=%fused_computation.577 | convolution fusion | flops 305332160 | bytes 10227584 | tf_op jit(solution)/shard_map/dot_general | solution.py:52
  381.6 2.5 convolution_convert_fusion.5
  390.0 3.2 convolution_convert_fusion.3
  393.3 3.5 fusion.93
  402.7 2.3 fusion.64
  410.9 17.0 %fusion.277 = (f32[512]{0:T(512)S(1)}, f32[512]{0:T(512)S(1)}, f32[512,768]{0,1:T(8,128)}) fusion(f32[512]{0:T(512)} %copy-done.112, f32[512,768]{0,1:T(8,128)} %copy-done.11, f32[512]{0:T(512)S(1)} %copy-done.103, f32[768]{0:T(1024)S(1)} %copy-done.97, f32[512,768]{0,1:T(8,128)} %convolution_add_fusion, ...), kind=kOutput, calls=%fused_computation.576 | convolution fusion | flops 4885314560 | bytes 22031360 | tf_op jit(solution)/shard_map/dot_general | solution.py:52
  428.0 3.8 convolution_convert_fusion.2
  433.2 10.2 %multiply_reduce_fusion = (f32[12,512]{1,0:T(8,128)S(1)}, f32[12,512,512]{1,2,0:T(8,128)}) fusion(f32[12,512,512]{1,2,0:T(8,128)} %get-tuple-element.144, f32[12,512]{1,0:T(8,128)S(1)} %copy-done.49, bf16[512,12,64]{0,2,1:T(8,128)(2,1)S(1)} %bitcast.348, bf16[512,12,64]{0,2,1:T(8,128)(2,1)S(1)} %bitcast.347), kind=kOutput, calls=%fused_computation.18 | convolution fusion | flops 412084224 | bytes 26787840 | tf_op jit(solution)/shard_map/qhd,khd->hqk/dot_general | solution.py:172
  445.8 7.1 %multiply_convert_fusion = bf16[12,512,512]{1,2,0:T(8,128)(2,1)S(1)} fusion(f32[12,512,512]{1,2,0:T(8,128)} %get-tuple-element.167, f32[12,512,512]{1,2,0:T(8,128)S(1)} %bitcast.338, f32[12,512]{1,0:T(8,128)S(1)} %get-tuple-element.166, f32[12,512]{1,0:T(8,128)S(1)} %copy-done.49), kind=kLoop, calls=%fused_computation.17 | loop fusion | flops 12582912 | bytes 31506432 | tf_op jit(solution)/shard_map/convert_element_type | solution.py:60
  454.0 2.9 multiply_convert_fusion.7
  471.3 2.7 reshape.945
  474.1 4.7 copy.256
  479.7 2.8 reshape.943
  482.5 4.3 copy.255
  487.8 5.3 pad_maximum_fusion
  493.1 10.2 %reshape.952 = f32[16,46080]{1,0:T(8,128)} reshape(f32[320,48,48]{2,1,0:T(8,128)} %pad_maximum_fusion) | data formatting | bytes 5898240 | tf_op jit(solution)/shard_map/reshape | solution.py:405
  505.6 3.5 reshape.954
  509.1 4.2 copy.267
  513.3 3.8 reshape.956
  517.1 4.7 copy.268
  522.8 2.1 reshape.958
  525.0 2.3 copy.269
  527.3 2.6 convolution_add_fusion.9
  533.3 5.5 pad_maximum_fusion.1
  538.7 10.3 %reshape.962 = f32[16,46080]{1,0:T(8,128)} reshape(f32[320,48,48]{2,1,0:T(8,128)} %pad_maximum_fusion.1) | data formatting | bytes 5898240 | tf_op jit(solution)/shard_map/reshape | solution.py:405
  551.6 3.3 collective-permute-done
  557.1 3.1 reduce.46
  561.8 41.5 %all_to_all.61 = bf16[16,2,23094]{2,1,0:T(2,128)(2,1)} all-to-all(bf16[16,2,23094]{2,1,0:T(2,128)(2,1)S(1)} %reshape.1011), channel_id=1, replica_groups=mesh['dp'=16,'section'=2] {'dp'}, dimensions={0} | all-to-all | bytes 2956032 | tf_op jit(solution)/shard_map/all_to_all | solution.py:412
  603.3 10.0 %reshape.1012 = bf16[16,1,46188]{2,1,0:T(2,128)(2,1)S(1)} reshape(bf16[16,2,23094]{2,1,0:T(2,128)(2,1)} %all_to_all.61) | data formatting | bytes 2956032
  613.3 3.3 convert_reduce_fusion
  619.3 9.9 %all_to_all.62 = f32[32,1,2]{2,1,0:T(1,128)S(1)} all-to-all(f32[32,1,2]{2,1,0:T(1,128)S(1)} %broadcast_in_dim.116), channel_id=1, replica_groups=mesh['dp'=16,'section'=2] {'dp','section'}, dimensions={0} | all-to-all | bytes 512 | tf_op jit(solution)/shard_map/all_to_all | solution.py:418
  (578 shorter events, 163.8 us)
Async XLA Ops:
  7.2 624.8 %copy-start = (f32[1,20,48,48]{3,2,1,0:T(8,128)S(1)}, f32[1,20,48,48]{3,2,1,0:T(8,128)}, u32[]{:S(2)}) copy-start(f32[1,20,48,48]{3,2,1,0:T(8,128)} %param.39) | copy-start | bytes 552964
  7.2 96.7 %all-gather.15.cloned.1.call-start = ((), (), s32[]{:S(2)}) async-start(), calls=%async_computation.12 | async-start | bytes 6099456 | tf_op jit(solution)/shard_map/all_gather | solution.py:336
  10.2 153.1 %all-gather.7.cloned.1.call-start = ((), (), s32[]{:S(2)}) async-start(), calls=%async_computation.8 | async-start | bytes 10616832 | tf_op jit(solution)/shard_map/all_gather | solution.py:344
  11.0 179.2 %all-gather.9.cloned.1.call-start = ((), (), s32[]{:S(2)}) async-start(), calls=%async_computation.9 | async-start | bytes 3538944 | tf_op jit(solution)/shard_map/all_gather | solution.py:344
  11.8 6.8 %copy-start.144 = (s32[2,1,32]{2,1,0:T(1,128)S(1)}, s32[2,1,32]{2,1,0:T(1,128)}, u32[]{:S(2)}) copy-start(s32[2,1,32]{2,1,0:T(1,128)} %param.27) | copy-start | bytes 772
  11.8 186.6 %all-gather.11.cloned.1.call-start = ((), (), s32[]{:S(2)}) async-start(), calls=%async_computation.10 | async-start | bytes 14155776 | tf_op jit(solution)/shard_map/all_gather | solution.py:344
  45.3 39.9 %all-to-all-start.3 = ((bf16[16,48,768]{2,1,0:T(8,128)(2,1)}), bf16[16,48,768]{2,1,0:T(8,128)(2,1)S(1)}, u32[]{:S(2)}, u32[]{:S(2)}) async-start(bf16[16,48,768]{2,1,0:T(8,128)(2,1)} %bitcast.7), calls=%async_computation.3 | async-start | bytes 2359296 | tf_op jit(solution)/shard_map/all_to_all | solution.py:241
  49.0 5.8 copy-start.156
  49.0 157.3 %all-gather.13.cloned.1.call-start = ((), (), s32[]{:S(2)}) async-start(), calls=%async_computation.11 | async-start | bytes 14155776 | tf_op jit(solution)/shard_map/all_gather | solution.py:344
  54.2 118.6 %copy-start.157 = (pred[512]{0:T(512)(128)(4,1)}, pred[512]{0:T(512)(128)(4,1)S(1)}, u32[]{:S(2)}) copy-start(pred[512]{0:T(512)(128)(4,1)S(1)} %iota_compare_fusion.11) | copy-start | bytes 1540
  54.8 151.5 %copy-start.96 = (f32[768]{0:T(1024)}, f32[768]{0:T(1024)S(1)}, u32[]{:S(2)}) copy-start(f32[768]{0:T(1024)S(1)} %get-tuple-element.77) | copy-start | bytes 9220
  54.8 165.1 %copy-start.98 = (f32[768]{0:T(1024)}, f32[768]{0:T(1024)S(1)}, u32[]{:S(2)}) copy-start(f32[768]{0:T(1024)S(1)} %get-tuple-element.75) | copy-start | bytes 9220
  54.8 199.1 %copy-start.106 = (f32[768]{0:T(1024)}, f32[768]{0:T(1024)S(1)}, u32[]{:S(2)}) copy-start(f32[768]{0:T(1024)S(1)} %get-tuple-element.71) | copy-start | bytes 9220
  54.9 201.2 %copy-start.117 = (f32[768]{0:T(1024)}, f32[768]{0:T(1024)S(1)}, u32[]{:S(2)}) copy-start(f32[768]{0:T(1024)S(1)} %get-tuple-element.68) | copy-start | bytes 9220
  54.9 171.8 %copy-start.137 = (s32[32]{0:T(128)}, s32[32]{0:T(128)S(1)}, u32[]{:S(2)}) copy-start(s32[32]{0:T(128)S(1)} %fusion.205) | copy-start | bytes 388
  150.0 8.2 %copy-start.9 = (f32[512,768]{0,1:T(8,128)S(1)}, f32[512,768]{0,1:T(8,128)}, u32[]{:S(2)}) copy-start(f32[512,768]{0,1:T(8,128)} %multiply_add_fusion.6) | copy-start | bytes 4718596
  150.0 8.2 %copy-start.27 = (bf16[384,192]{0,1:T(8,128)(2,1)S(1)}, bf16[384,192]{0,1:T(8,128)(2,1)}, u32[]{:S(2)}) copy-start(bf16[384,192]{0,1:T(8,128)(2,1)} %reshape.919) | copy-start | bytes 442372
  160.8 29.4 %copy-start.3 = (f32[512,384]{0,1:T(8,128)}, f32[512,384]{0,1:T(8,128)S(1)}, u32[]{:S(2)}) copy-start(f32[512,384]{0,1:T(8,128)S(1)} %fusion.82) | copy-start | bytes 2359300
  170.9 12.6 %copy-start.7 = (bf16[512,768]{0,1:T(8,128)(2,1)}, bf16[512,768]{0,1:T(8,128)(2,1)S(1)}, u32[]{:S(2)}) copy-start(bf16[512,768]{0,1:T(8,128)(2,1)S(1)} %copy.234) | copy-start | bytes 2359300
  183.5 6.7 %copy-start.48 = (f32[12,512]{1,0:T(8,128)}, f32[12,512]{1,0:T(8,128)S(1)}, u32[]{:S(2)}) copy-start(f32[12,512]{1,0:T(8,128)S(1)} %broadcast_divide_fusion) | copy-start | bytes 73732
  192.8 13.5 %copy-start.102 = (f32[512]{0:T(512)}, f32[512]{0:T(512)S(1)}, u32[]{:S(2)}) copy-start(f32[512]{0:T(512)S(1)} %broadcast_multiply_fusion.5) | copy-start | bytes 6148
  194.2 12.2 %copy-start.112 = (f32[512]{0:T(512)}, f32[512]{0:T(512)S(1)}, u32[]{:S(2)}) copy-start(f32[512]{0:T(512)S(1)} %add_rsqrt_fusion.1) | copy-start | bytes 6148
  224.3 7.7 %copy-start.158 = (pred[512]{0:T(512)(128)(4,1)S(1)}, pred[512]{0:T(512)(128)(4,1)}, u32[]{:S(2)}) copy-start(pred[512]{0:T(512)(128)(4,1)} %copy-done.157) | copy-start | bytes 1540
  249.4 5.3 copy-start.87
  253.0 39.3 %copy-start.77 = (f32[32,768]{1,0:T(8,128)}, f32[32,768]{1,0:T(8,128)S(1)}, u32[]{:S(2)}) copy-start(f32[32,768]{1,0:T(8,128)S(1)} %fusion.101) | copy-start | bytes 294916
  253.4 39.0 %copy-start.80 = (f32[32,384]{1,0:T(8,128)}, f32[32,384]{1,0:T(8,128)S(1)}, u32[]{:S(2)}) copy-start(f32[32,384]{1,0:T(8,128)S(1)} %convolution_add_fusion.21) | copy-start | bytes 147460
  254.5 51.9 %slice-start = ((s8[11476992]{0:T(1024)(128)(4,1)}), s8[4194304]{0:T(1024)(128)(4,1)S(1)}, s32[]{:S(2)}) async-start(s8[11476992]{0:T(1024)(128)(4,1)} %bitcast.335), calls=%async_computation.13 | async-start | bytes 8388608
  255.8 50.5 %copy-start.128 = (f32[32]{0:T(128)}, f32[32]{0:T(128)S(1)}, u32[]{:S(2)}) copy-start(f32[32]{0:T(128)S(1)} %add_multiply_fusion.1) | copy-start | bytes 388
  292.4 14.0 %slice-start.1 = ((s8[11476992]{0:T(1024)(128)(4,1)}), s8[4194304]{0:T(1024)(128)(4,1)S(1)}, s32[]{:S(2)}) async-start(s8[11476992]{0:T(1024)(128)(4,1)} %bitcast.335), calls=%async_computation.14 | async-start | bytes 8388608
  292.4 14.0 %slice-start.2 = ((s8[11476992]{0:T(1024)(128)(4,1)}), s8[3088384]{0:T(1024)(128)(4,1)S(1)}, s32[]{:S(2)}) async-start(s8[11476992]{0:T(1024)(128)(4,1)} %bitcast.335), calls=%async_computation.15 | async-start | bytes 6176768
  330.6 24.9 %all-to-all-start.5 = ((bf16[16,32,896]{2,1,0:T(8,128)(2,1)}), bf16[16,32,896]{2,1,0:T(8,128)(2,1)}, u32[]{:S(2)}, u32[]{:S(2)}) async-start(bf16[16,32,896]{2,1,0:T(8,128)(2,1)} %bitcast.364), calls=%async_computation.5 | async-start | bytes 1835008 | tf_op jit(solution)/shard_map/all_to_all | solution.py:287
  359.5 6.5 %copy-start.84 = (bf16[192,384]{1,0:T(8,128)(2,1)S(1)}, bf16[192,384]{1,0:T(8,128)(2,1)}, u32[]{:S(2)}) copy-start(bf16[192,384]{1,0:T(8,128)(2,1)} %reshape.921) | copy-start | bytes 442372
  359.5 6.5 %copy-start.94 = (f32[32,192]{1,0:T(8,128)S(1)}, f32[32,192]{1,0:T(8,128)}, u32[]{:S(2)}) copy-start(f32[32,192]{1,0:T(8,128)} %copy-done.93) | copy-start | bytes 73732
  359.5 7.3 %copy-start.29 = (bf16[384,192]{0,1:T(8,128)(2,1)S(1)}, bf16[384,192]{0,1:T(8,128)(2,1)}, u32[]{:S(2)}) copy-start(bf16[384,192]{0,1:T(8,128)(2,1)} %reshape.919) | copy-start | bytes 442372
  359.5 8.0 %copy-start.88 = (bf16[192,384]{1,0:T(8,128)(2,1)S(1)}, bf16[192,384]{1,0:T(8,128)(2,1)}, u32[]{:S(2)}) copy-start(bf16[192,384]{1,0:T(8,128)(2,1)} %reshape.925) | copy-start | bytes 442372
  359.5 8.0 %copy-start.91 = (f32[32,192]{1,0:T(8,128)S(1)}, f32[32,192]{1,0:T(8,128)}, u32[]{:S(2)}) copy-start(f32[32,192]{1,0:T(8,128)} %copy-done.90) | copy-start | bytes 73732
  359.5 8.8 %copy-start.22 = (bf16[384,192]{0,1:T(8,128)(2,1)S(1)}, bf16[384,192]{0,1:T(8,128)(2,1)}, u32[]{:S(2)}) copy-start(bf16[384,192]{0,1:T(8,128)(2,1)} %reshape.923) | copy-start | bytes 442372
  359.5 8.9 %copy-start.36 = (f32[32,768]{1,0:T(8,128)S(1)}, f32[32,768]{1,0:T(8,128)}, u32[]{:S(2)}) copy-start(f32[32,768]{1,0:T(8,128)} %copy-done.35) | copy-start | bytes 294916
  359.5 8.9 %copy-start.107 = (f32[768]{0:T(1024)S(1)}, f32[768]{0:T(1024)}, u32[]{:S(2)}) copy-start(f32[768]{0:T(1024)} %copy-done.106) | copy-start | bytes 9220
  359.5 8.9 %copy-start.127 = (f32[32]{0:T(128)S(1)}, f32[32]{0:T(128)}, u32[]{:S(2)}) copy-start(f32[32]{0:T(128)} %copy-done.126) | copy-start | bytes 388
  359.5 8.9 %copy-start.135 = (f32[32]{0:T(128)S(1)}, f32[32]{0:T(128)}, u32[]{:S(2)}) copy-start(f32[32]{0:T(128)} %copy-done.134) | copy-start | bytes 388
  359.5 9.8 %copy-start.62 = (bf16[384,768]{1,0:T(8,128)(2,1)S(1)}, bf16[384,768]{1,0:T(8,128)(2,1)}, u32[]{:S(2)}) copy-start(bf16[384,768]{1,0:T(8,128)(2,1)} %reshape.939) | copy-start | bytes 1769476
  359.5 9.8 %copy-start.81 = (f32[32,384]{1,0:T(8,128)S(1)}, f32[32,384]{1,0:T(8,128)}, u32[]{:S(2)}) copy-start(f32[32,384]{1,0:T(8,128)} %copy-done.80) | copy-start | bytes 147460
  361.0 9.8 %copy-start.18 = (bf16[768,384]{1,0:T(8,128)(2,1)S(1)}, bf16[768,384]{1,0:T(8,128)(2,1)}, u32[]{:S(2)}) copy-start(bf16[768,384]{1,0:T(8,128)(2,1)} %reshape.937) | copy-start | bytes 1769476
  362.7 9.1 %copy-start.124 = (f32[768]{0:T(1024)S(1)}, f32[768]{0:T(1024)}, u32[]{:S(2)}) copy-start(f32[768]{0:T(1024)} %get-tuple-element.73) | copy-start | bytes 9220
  362.7 9.1 %copy-start.132 = (f32[32]{0:T(128)S(1)}, f32[32]{0:T(128)}, u32[]{:S(2)}) copy-start(f32[32]{0:T(128)} %copy-done.131) | copy-start | bytes 388
  380.4 7.3 %copy-start.159 = (f32[32]{0:T(128)}, f32[32]{0:T(128)S(1)}, u32[]{:S(2)}) copy-start(f32[32]{0:T(128)S(1)} %broadcast_multiply_fusion.7) | copy-start | bytes 388
  390.0 9.1 %copy-start.133 = (f32[32]{0:T(128)S(1)}, f32[32]{0:T(128)}, u32[]{:S(2)}) copy-start(f32[32]{0:T(128)} %copy-done.131) | copy-start | bytes 388
  396.7 5.9 copy-start.99
  396.8 5.9 copy-start.105
  396.8 5.9 copy-start.115
  410.9 17.1 %copy-start.13 = (f32[512,768]{0,1:T(8,128)S(1)}, f32[512,768]{0,1:T(8,128)}, u32[]{:S(2)}) copy-start(f32[512,768]{0,1:T(8,128)} %copy-done.11) | copy-start | bytes 4718596
  410.9 17.1 %copy-start.113 = (f32[512]{0:T(512)S(1)}, f32[512]{0:T(512)}, u32[]{:S(2)}) copy-start(f32[512]{0:T(512)} %copy-done.112) | copy-start | bytes 6148
  433.1 10.3 %slice-start.3 = ((s8[12582912]{0:T(1024)(128)(4,1)}), s8[4194304]{0:T(1024)(128)(4,1)S(1)}, s32[]{:S(2)}) async-start(s8[12582912]{0:T(1024)(128)(4,1)} %bitcast.337), calls=%async_computation.16 | async-start | bytes 8388608
  433.2 11.4 %slice-start.4 = ((s8[12582912]{0:T(1024)(128)(4,1)}), s8[4194304]{0:T(1024)(128)(4,1)S(1)}, s32[]{:S(2)}) async-start(s8[12582912]{0:T(1024)(128)(4,1)} %bitcast.337), calls=%async_computation.17 | async-start | bytes 8388608
  433.2 12.6 %slice-start.5 = ((s8[12582912]{0:T(1024)(128)(4,1)}), s8[4194304]{0:T(1024)(128)(4,1)S(1)}, s32[]{:S(2)}) async-start(s8[12582912]{0:T(1024)(128)(4,1)} %bitcast.337), calls=%async_computation.18 | async-start | bytes 8388608
  445.8 7.1 %copy-start.8 = (bf16[512,768]{0,1:T(8,128)(2,1)S(1)}, bf16[512,768]{0,1:T(8,128)(2,1)}, u32[]{:S(2)}) copy-start(bf16[512,768]{0,1:T(8,128)(2,1)} %copy-done.7) | copy-start | bytes 2359300
  454.0 8.1 %slice-start.6 = ((s8[7077888]{0:T(1024)(128)(4,1)}), s8[2883584]{0:T(1024)(128)(4,1)S(1)}, s32[]{:S(2)}) async-start(s8[7077888]{0:T(1024)(128)(4,1)} %bitcast.350), calls=%async_computation.19 | async-start | bytes 5767168
  464.3 5.7 copy-start.42
  465.0 5.4 copy-start.50
  551.6 3.3 collective-permute-start
  617.3 16.6 %copy-start.31 = (f32[1,20,48,48]{3,2,1,0:T(8,128)S(1)}, f32[1,20,48,48]{3,2,1,0:T(8,128)}, u32[]{:S(2)}) copy-start(f32[1,20,48,48]{3,2,1,0:T(8,128)} %param.35) | copy-start | bytes 552964
  617.3 16.6 %copy-start.63 = (f32[1,20,48,48]{3,2,1,0:T(8,128)S(1)}, f32[1,20,48,48]{3,2,1,0:T(8,128)}, u32[]{:S(2)}) copy-start(f32[1,20,48,48]{3,2,1,0:T(8,128)} %param.40) | copy-start | bytes 552964
  632.0 6.8 %copy-start.30 = (f32[1,20,48,48]{3,2,1,0:T(8,128)}, f32[1,20,48,48]{3,2,1,0:T(8,128)S(1)}, u32[]{:S(2)}) copy-start(f32[1,20,48,48]{3,2,1,0:T(8,128)S(1)} %mul.1102) | copy-start | bytes 552964
  (117 other events, 308.2 us)
Sparse Core Ops, SparseCore 0:
  11.6 85.0 all-gather.14
  98.3 17.4 all-gather.6
  117.4 12.1 all-gather.8
  130.9 23.0 all-gather.10
  155.4 23.0 all-gather.12

commit v2 on v1

--- a/solution.py
+++ b/solution.py
@@ -2,6 +2,8 @@
 import jax.numpy as jnp
 import numpy as np
 from jax import lax
+from jax.experimental import pallas as pl
+from jax.experimental.pallas import tpu as pltpu
 from jax.sharding import PartitionSpec as P
 
 D = 768
@@ -198,6 +200,219 @@
     attended_grad = summed_grad + matmul_t(inner_grad, w_up)
     start_grad = norm_back(attended_grad, kept_one, gains[0])
     return start_grad, low(matmul_t(low(start_grad), w_out)), adapter_grads
+
+
+GROUP_ROWS = 72
+LANES = 128
+
+
+def whole(shape):
+    return pl.BlockSpec(shape, lambda *_: (0,) * len(shape))
+
+
+def section_of(shape, section):
+    return pl.BlockSpec((None,) + shape, lambda *_: (section,) + (0,) * len(shape))
+
+
+def params_for(mebibytes):
+    return pltpu.CompilerParams(vmem_limit_bytes=mebibytes * 2**20)
+
+
+def roll(values, shift):
+    return pltpu.roll(values, shift, 1)
+
+
+def lane_of(values):
+    return lax.broadcasted_iota(jnp.int32, values.shape, 1)
+
+
+def fold_half(values, upper):
+    top, bottom = values[:24], values[24:]
+    if upper:
+        return jnp.where(lane_of(top) < 64, roll(top, 64), bottom)
+    return jnp.where(lane_of(top) < 64, top, roll(bottom, 64))
+
+
+def unfold_half(values, upper):
+    turned = roll(values, 64)
+    return jnp.concatenate([turned, values] if upper else [values, turned], 0)
+
+
+def join_pair(main_0, rest_0, main_1, rest_1):
+    left = lane_of(main_0) < 64
+    turned = roll(main_1, 64)
+    return (
+        main_0,
+        jnp.where(left, unfold_half(rest_0, False), turned),
+        jnp.where(left, turned, unfold_half(rest_1, True)),
+    )
+
+
+def cut_pair(tile_0, tile_1, tile_2):
+    left = lane_of(tile_0) < 64
+    return (
+        (tile_0, fold_half(tile_1, False)),
+        (jnp.where(left, roll(tile_1, 64), roll(tile_2, 64)), fold_half(tile_2, True)),
+    )
+
+
+def chunk_rows(own_blocks):
+    return own_blocks // 4 * GROUP_ROWS + 8
+
+
+def pack_own(master, bias_rows):
+    count = master.shape[0]
+
+    def kernel(master_ref, bias_ref, out_ref):
+        row = lax.broadcasted_iota(jnp.int32, (BLOCK, 256), 0)
+        col = lax.broadcasted_iota(jnp.int32, (BLOCK, 256), 1)
+        pieces = []
+        for group in range(count // 4):
+            wide = jnp.zeros((BLOCK, 256), F32)
+            for j in range(4):
+                wide += matmul(low(master_ref[4 * group + j]), (col == row + BLOCK * j).astype(BF16))
+            pieces += [wide[:, :LANES], fold_half(wide[:, LANES:], False)]
+        out_ref[...] = low(jnp.concatenate(pieces + [bias_ref[...]], 0))
+
+    return pl.pallas_call(
+        kernel,
+        out_shape=jax.ShapeDtypeStruct((chunk_rows(count), LANES), BF16),
+        name="pack_own",
+    )(master, bias_rows)
+
+
+MATRICES = ((D, BOT), (BOT, D), (HALF, INV_H), (INV_H, HALF))
+
+
+def unpack_all(gathered):
+    sections, parts, rows, _ = gathered.shape
+    per_part = (rows - 8) // GROUP_ROWS
+
+    def kernel(in_ref, *out_refs):
+        cache = {}
+
+        def group(index):
+            part = index // per_part
+            if part not in cache:
+                cache.clear()
+                cache[part] = in_ref[part].astype(F32)
+            base = index % per_part * GROUP_ROWS
+            chunk = cache[part]
+            return chunk[base : base + BLOCK], chunk[base + BLOCK : base + GROUP_ROWS]
+
+        index = 0
+        for (height, width), out_ref in zip(MATRICES, out_refs):
+            for top in range(0, height, BLOCK):
+                if width == INV_H:
+                    main, rest = group(index)
+                    index += 1
+                    out_ref[top : top + BLOCK, :LANES] = low(main)
+                    out_ref[top : top + BLOCK, LANES:] = low(unfold_half(rest, False)[:, :64])
+                    continue
+                for left in range(0, width, HALF):
+                    tiles = join_pair(*group(index), *group(index + 1))
+                    index += 2
+                    for j, tile in enumerate(tiles):
+                        at = left + j * LANES
+                        out_ref[top : top + BLOCK, at : at + LANES] = low(tile)
+
+    return pl.pallas_call(
+        kernel,
+        grid=(sections,),
+        in_specs=[pl.BlockSpec((None, parts, rows, LANES), lambda s: (s, 0, 0, 0))],
+        out_specs=[pl.BlockSpec((None,) + shape, lambda s: (s, 0, 0)) for shape in MATRICES],
+        out_shape=[jax.ShapeDtypeStruct((sections,) + shape, BF16) for shape in MATRICES],
+        compiler_params=params_for(32),
+        name="unpack_all",
+    )(gathered)
+
+
+def pack_grads(grads, bias_rows, own_index, parts):
+    per_part = 80 // parts
+    rows = per_part * GROUP_ROWS + 8
+
+    def kernel(index_ref, *refs):
+        bias_ref, own_ref, other_ref = refs[8:]
+        own = index_ref[0]
+        for section in range(MICRO):
+            pieces = []
+            for (height, width), ref in zip(MATRICES, refs[4 * section : 4 * section + 4]):
+                for top in range(0, height, BLOCK):
+                    band = slice(top, top + BLOCK)
+                    if width == INV_H:
+                        tail = ref[band, LANES:]
+                        tail = jnp.concatenate([tail, tail], 1)
+                        pieces.append((ref[band, :LANES], fold_half(tail, False)))
+                        continue
+                    for left in range(0, width, HALF):
+                        tiles = [ref[band, left + j * LANES : left + (j + 1) * LANES] for j in range(3)]
+                        pieces += cut_pair(*tiles)
+                while len(pieces) >= per_part:
+                    part = sum_done[section]
+                    sum_done[section] += 1
+                    chunk = [half for pair in pieces[:per_part] for half in pair]
+                    del pieces[:per_part]
+                    chunk = jnp.concatenate(chunk + [bias_ref[section, part]], 0)
+
+                    @pl.when(own == section)
+                    def _(part=part, chunk=chunk):
+                        own_ref[part] = chunk
+
+                    @pl.when(own != section)
+                    def _(part=part, chunk=chunk):
+                        other_ref[part] = low(chunk)
+
+    sum_done = [0, 0]
+    return pl.pallas_call(
+        kernel,
+        in_specs=[pl.BlockSpec(memory_space=pltpu.SMEM)] + [pl.BlockSpec(memory_space=pltpu.VMEM)] * 9,
+        out_shape=[
+            jax.ShapeDtypeStruct((parts, rows, LANES), F32),
+            jax.ShapeDtypeStruct((parts, rows, LANES), BF16),
+        ],
+        compiler_params=params_for(40),
+        name="pack_grads",
+    )(own_index, *grads[0], *grads[1], bias_rows)
+
+
+def sum_owned(came, loss_part, copies):
+    parts, rows, _ = came.shape
+    per_part = (rows - 8) // GROUP_ROWS
+
+    def kernel(loss_ref, came_ref, blocks_ref, bias_ref, pair_ref):
+        total = came_ref[0].astype(F32)
+        for part in range(1, parts):
+            total += came_ref[part].astype(F32)
+        for group in range(per_part):
+            base = group * GROUP_ROWS
+            main = total[base : base + BLOCK]
+            rest = unfold_half(total[base + BLOCK : base + GROUP_ROWS], False)
+            lane = lane_of(main)
+            parts_of = (
+                main,
+                roll(main, 80),
+                jnp.where(lane < 32, roll(main, 32), roll(rest, 32)),
+                roll(rest, 112),
+            )
+            for j, values in enumerate(parts_of):
+                blocks_ref[4 * group + j] = values[:, :BLOCK]
+        bias_ref[...] = total[rows - 8 :]
+        squares = jnp.sum(jnp.sum(total * total, 0, keepdims=True), 1, keepdims=True)
+        lane = lax.broadcasted_iota(jnp.int32, (1, LANES), 1)
+        pair = jnp.where(lane == 0, squares, jnp.where(lane == 1, loss_ref[0], 0.0))
+        pair_ref[...] = jnp.broadcast_to(pair[None], pair_ref.shape)
+
+    return pl.pallas_call(
+        kernel,
+        in_specs=[pl.BlockSpec(memory_space=pltpu.SMEM), pl.BlockSpec(memory_space=pltpu.VMEM)],
+        out_shape=[
+            jax.ShapeDtypeStruct((4 * per_part, BLOCK, BLOCK), F32),
+            jax.ShapeDtypeStruct((8, LANES), F32),
+            jax.ShapeDtypeStruct((copies, 1, LANES), F32),
+        ],
+        compiler_params=params_for(32),
+        name="sum_owned",
+    )(loss_part, came)
 
 
 def swap_add(own, other):
@@ -294,6 +509,64 @@
     loss = jnp.sum(row_weights * (top + jnp.log(total) - target_logit))
     expected = jnp.sum(came[:, :, :D] * (factor / total)[:, :, None], 0)
     return loss, (row_weights / weight_sum)[:, None] * (expected - target_rows)
+
+
+def bias_chunks(vector, parts):
+    rows = vector.reshape(-1, parts, 1, vector.shape[-1] // parts)
+    return jnp.pad(rows, ((0, 0), (0, 0), (0, 7), (0, LANES - rows.shape[-1])))
+
+
+def gather_params(master, vector):
+    parts = lax.axis_size("dp")
+    count, width = master.shape[0], vector.shape[0]
+    if count % 4 == 0 and width <= LANES:
+        packed = pack_own(master, bias_chunks(vector, 1)[0, 0])
+        gathered = lax.all_gather(packed, ("section", "dp")).reshape(MICRO, parts, -1, LANES)
+        vectors = gathered[:, :, -8, :width].reshape(MICRO, parts * width)
+        matrices = unpack_all(gathered)
+        params = []
+        for s in range(MICRO):
+            down, up, c_down, c_up = (matrix[s] for matrix in matrices)
+            bias = vectors[s]
+            adapter = (down, bias[:BOT], up, bias[BOT : BOT + D])
+            coupling = (c_down, bias[BOT + D : BOT + D + INV_H], c_up, bias[BOT + D + INV_H :])
+            params.append((adapter, coupling))
+    else:
+        flat = low(jnp.concatenate([master.reshape(-1), vector]))
+        gathered = lax.all_gather(flat, ("section", "dp")).reshape(MICRO, parts, -1)
+        size = count * BLOCK**2
+        all_blocks = gathered[:, :, :size].reshape(MICRO, parts * count, BLOCK, BLOCK)
+        all_vectors = gathered[:, :, size:].reshape(MICRO, parts * width)
+        params = [split_params(all_blocks[s], all_vectors[s]) for s in range(MICRO)]
+    return [pair[0] for pair in params], params[0][1], params[1][1]
+
+
+def sum_at_owners(grads, loss_part, count):
+    parts = lax.axis_size("dp")
+    section = lax.axis_index("section")
+    width = (BOT + D + INV_H + HALF) // parts
+    if count % 4 == 0 and width <= LANES:
+        matrices = [(a[0], a[2], c[0], c[2]) for a, c in grads]
+        biases = jnp.stack([jnp.concatenate([a[1], a[3], c[1], c[3]]) for a, c in grads])
+        own, other = pack_grads(
+            matrices, bias_chunks(biases, parts), section.reshape(1).astype(jnp.int32), parts
+        )
+        came = lax.all_to_all(low(swap_add(own, other)), "dp", 0, 0)
+        blocks, bias, pair = sum_owned(came, loss_part.reshape(1), parts * MICRO)
+        return blocks, bias[0, :width], pair
+    flat = []
+    for adapter, coupling in grads:
+        blocks, vector = join_params(adapter, coupling)
+        flat.append(
+            jnp.concatenate([blocks.reshape(parts, count * BLOCK**2), vector.reshape(parts, width)], 1)
+        )
+    first = section == 0
+    summed = swap_add(jnp.where(first, flat[0], flat[1]), jnp.where(first, flat[1], flat[0]))
+    owned = jnp.sum(lax.all_to_all(low(summed), "dp", 0, 0).astype(F32), 0)
+    blocks = owned[: count * BLOCK**2].reshape(count, BLOCK, BLOCK)
+    pair = jnp.stack([jnp.sum(owned * owned), loss_part])
+    pair = jnp.broadcast_to(pair[None, None], (parts * MICRO, 1, 2))
+    return blocks, owned[count * BLOCK**2 :], pair
 
 
 def shards(
@@ -330,15 +603,7 @@
     spots = pick(first_section, positions[:, 0])
     row_weights = pick(first_section, loss_weights[:, 0]).astype(F32)
 
-    own_blocks = master.shape[1]
-    own_vector = vectors.shape[1]
-    flat = low(jnp.concatenate([master[0].reshape(-1), vectors[0]]))
-    gathered = lax.all_gather(flat, ("section", "dp")).reshape(MICRO, parts, -1)
-    all_blocks = gathered[:, :, : own_blocks * BLOCK**2].reshape(MICRO, parts * own_blocks, BLOCK, BLOCK)
-    all_vectors = gathered[:, :, own_blocks * BLOCK**2 :].reshape(MICRO, parts * own_vector)
-    params = [split_params(all_blocks[s], all_vectors[s]) for s in range(MICRO)]
-    adapters = [pair[0] for pair in params]
-    coupling_one, coupling_two = (pair[1] for pair in params)
+    adapters, coupling_one, coupling_two = gather_params(master[0], vectors[0])
     norms = lax.all_gather(norm_params, "section", axis=0, tiled=True)
     w_qkv, w_out, w_up, w_down = (
         lax.all_gather(weight, "section", axis=0, tiled=True)
@@ -399,23 +664,10 @@
     grads_one = jax.tree.map(jnp.add, grads_one, first_one)
     grads_two = jax.tree.map(jnp.add, grads_two, first_two)
 
-    joined = [join_params(adapter_grads_0, grads_one), join_params(adapter_grads_1, grads_two)]
-    flat = [
-        jnp.concatenate(
-            [blocks.reshape(parts, own_blocks * BLOCK**2), vector.reshape(parts, own_vector)], 1
-        )
-        for blocks, vector in joined
-    ]
-    summed = swap_add(
-        jnp.where(first_section, flat[0], flat[1]), jnp.where(first_section, flat[1], flat[0])
-    )
-    owned = jnp.sum(lax.all_to_all(low(summed), "dp", 0, 0).astype(F32), 0)
-    grad_blocks = owned[: own_blocks * BLOCK**2].reshape(own_blocks, BLOCK, BLOCK)
-    grad_vector = owned[own_blocks * BLOCK**2 :]
-
-    squares = jnp.sum(owned * owned)
-    pair = jnp.broadcast_to(jnp.stack([squares, loss_part])[None], (parts * MICRO, 2))
-    totals = jnp.sum(lax.all_to_all(pair, ("dp", "section"), 0, 0), 0)
+    grad_blocks, grad_vector, pair = sum_at_owners(
+        ((adapter_grads_0, grads_one), (adapter_grads_1, grads_two)), loss_part, master.shape[1]
+    )
+    totals = jnp.sum(lax.all_to_all(pair, ("dp", "section"), 0, 0), (0, 1))
     grad_norm = jnp.sqrt(totals[0])
     loss_sum = totals[1]
     factor = CLIP_NORM / jnp.maximum(grad_norm, CLIP_NORM)

time: 653 us -> 522 us (0.80)
  local copies, waits for them, and re-layouts: 184 us -> 74.9 us
  other arithmetic: 73.6 us -> 52.5 us
  loops' own time: 12.6 us -> 0.86 us
  Pallas kernels: 0 us -> 7.68 us
  matrix products: 189 us -> 196 us
    reshape x36 -> x0, local copies, waits for them, and re-layouts: 83.5 us -> none  [the longest x16 39.6 us: to_blocks(): matrix.reshape(rows_in // BLOCK, BLOCK, cols_in // BLOCK, BLOCK)]
    slice x7 -> x2, local copies, waits for them, and re-layouts: 13.4 us -> 1.31 us  [the longest x1 0.66 us: rest_fwd(): result, kept_two = layer_norm(summed + branch_out, gains[2], gains[3])]
    another operation x1, loops' own time: 12.6 us -> 0.86 us  [fetch_rows(): lax.while_loop(more, another, (jnp.int32(1), rows))[1]]
    unnamed x354 -> x349, local copies, waits for them, and re-layouts: 33.9 us -> 22.7 us
    concatenate x2 -> x0, other arithmetic: 10.8 us -> none  [join_params(): jnp.concatenate([to_blocks(adapter[0]), to_blocks(adapter[2]), to_blocks(...]
    squeeze x4 -> x3, local copies, waits for them, and re-layouts: 13 us -> 3.47 us  [the longest x2 2.17 us: gather_params(): bias = vectors[s]]
    pallas_call x0 -> x4, Pallas kernels: none -> 7.68 us  [the longest x1 2.41 us: unpack_all(): pl.pallas_call(kernel, grid=(sections,), in_specs=[pl.BlockSpec((None, pa...]
  transfers between devices with their start and end apart: 8 -> 8, of which waited for: 3 -> 3; matrix products, arithmetic and copies ran while one was open for 19% -> 17% of each run, Pallas kernels for 0% -> 0%
where the time goes in v2:
time: 522 us; the launch traced here: 513 us
  matrix products  196 us (38%)
  blocking collectives  97.4 us (19%)
  local copies, waits for them, and re-layouts  74.9 us (14%)
  other arithmetic  52.5 us (10%)
  waiting for transfers between devices  51.9 us (10%)
  between operations  23.3 us (4%)
  starting transfers between devices  8.69 us (2%)
  Pallas kernels  7.68 us (1%)
    dot_general x20, matrix products, matmul_t(): lax.dot_general(left, right, (((1,), (1,)), ((), ())), preferred_element_...  63.6 us
    dot_general x24, matrix products, matmul(): return jnp.dot(left, right, preferred_element_type=F32)  63.2 us
    all_to_all x1, blocking collectives, sum_at_owners(): came = lax.all_to_all(low(swap_add(own, other)), 'dp', 0, 0)  42 us
    all_to_all x1, blocking collectives, head(): lax.all_to_all(jnp.broadcast_to(mine[None], (parts, COUNT, D)), 'dp', 0, 0)  28.5 us
    all_to_all x1, waiting for transfers between devices, answer(): came = lax.all_to_all(rows, 'dp', 0, 0).reshape(parts * slots, D)  26.3 us
    unnamed x349, local copies, waits for them, and re-layouts  22.7 us
    all_to_all x1, waiting for transfers between devices, head(): came = lax.all_to_all(packed, 'dp', 0, 0).astype(F32)  19.8 us
    all_to_all x1, blocking collectives, fetch_rows(): lax.all_to_all(jnp.concatenate([wanted(hits), extra], 1), 'dp', 0, 0)  15.4 us
  transfers between devices with their start and end apart: 8, of which 3 were waited for; matrix products, arithmetic and copies ran while one was open for 17% of the time, Pallas kernels for 0%

profile of v2, /device:TPU:0, one launch (start us, length us, event | category | flops | bytes accessed | tf_op | source)
XLA Modules:
  0.0 513.4 jit_solution(14064106360466777170)
XLA Ops:
  8.5 2.0 pack_own.1
  20.4 15.4 %all_to_all.54 = s32[16,1,50]{2,1,0:T(1,128)S(1)} all-to-all(s32[16,1,50]{2,1,0:T(1,128)S(1)} %bitcast.325), channel_id=1, replica_groups=mesh['dp'=16,'section'=2] {'dp'}, dimensions={0} | all-to-all | bytes 6400 | tf_op jit(solution)/shard_map/all_to_all | solution.py:461
  35.9 9.8 %gather_fusion.1 = bf16[768,768]{1,0:T(8,128)(2,1)} fusion(bf16[7472,768]{1,0:T(8,128)(2,1)} %param.28, s32[1024]{0:T(1024)S(1)} %pad_clamp_fusion.1), kind=kCustom, calls=%fused_computation.1 | custom fusion | bytes 2362368 | tf_op jit(solution)/shard_map/gather | solution.py:455
  45.7 3.7 all-to-all-start.3
  52.8 1.8 all_gather.21
  57.0 26.3 %all-to-all-done.3 = bf16[16,48,768]{2,1,0:T(8,128)(2,1)S(1)} async-done(((bf16[16,48,768]{2,1,0:T(8,128)(2,1)}), bf16[16,48,768]{2,1,0:T(8,128)(2,1)S(1)}, u32[]{:S(2)}, u32[]{:S(2)}) %all-to-all-start.3) | async-done | bytes 1179680 | tf_op jit(solution)/shard_map/all_to_all | solution.py:456
  83.3 2.1 fusion.61
  86.3 1.8 copy.181
  90.2 2.4 copy-done.2
  92.6 2.4 unpack_all.1
  103.8 1.9 fusion.81
  109.3 5.1 convolution_convert_fusion
  115.8 2.4 copy.185
  118.2 2.3 copy.186
  120.5 2.3 copy.184
  122.8 13.1 %fusion.329 = (f32[12,512]{1,0:T(8,128)}, f32[12,512,512]{1,2,0:T(8,128)}) fusion(pred[512]{0:T(512)(128)(4,1)S(1)} %copy-done.159, bf16[512,12,64]{0,2,1:T(8,128)(2,1)} %bitcast.310, bf16[512,12,64]{0,2,1:T(8,128)(2,1)} %bitcast.304), kind=kOutput, calls=%fused_computation.612 | convolution fusion | flops 415236608 | bytes 14180864 | tf_op jit(solution)/shard_map/sub | solution.py:166
  137.3 6.9 %fusion.73 = bf16[12,64,512]{2,1,0:T(8,128)(2,1)} fusion(bf16[512,12,64]{0,2,1:T(8,128)(2,1)} %bitcast.296, f32[12,512,512]{1,2,0:T(8,128)} %get-tuple-element.154, f32[12,512]{1,0:T(8,128)S(1)} %broadcast_divide_fusion), kind=kOutput, calls=%fused_computation.134 | convolution fusion | flops 409337856 | bytes 14180352 | tf_op jit(solution)/shard_map/hqk,khd->qhd/dot_general | solution.py:168
  144.3 2.8 fusion.330
  149.0 4.8 slice_bitcast_fusion.12
  153.8 9.3 %fusion.18 = f32[512,3072]{1,0:T(8,128)} fusion(bf16[2,768,3072]{2,1,0:T(8,128)(2,1)} %all-gather.11.cloned.1.call-done, f32[512,768]{0,1:T(8,128)} %copy-done.20, f32[768]{0:T(1024)S(1)} %get-tuple-element.96, f32[768]{0:T(1024)S(1)} %get-tuple-element.97, f32[512]{0:T(512)} %add_rsqrt_fusion.1, f32[512]{0:T(512)S(1)} %broadcast_multiply_fusion.5), kind=kOutput, calls=%fused_computation.46 | convolution fusion | flops 2417885184 | bytes 12593152 | tf_op jit(solution)/shard_map/dot_general | solution.py:50
  163.1 11.0 %fusion.65 = f32[512,768]{0,1:T(8,128)S(1)} fusion(bf16[2,3072,768]{2,1,0:T(8,128)(2,1)} %all-gather.13.cloned.1.call-done, f32[512,3072]{1,0:T(8,128)} %fusion.18, f32[512,768]{0,1:T(8,128)} %copy-done.20, f32[768]{0:T(1024)S(1)} %get-tuple-element.96, f32[768]{0:T(1024)S(1)} %get-tuple-element.97, f32[512]{0:T(512)} %add_rsqrt_fusion.1, ...), kind=kOutput, calls=%fused_computation.129 | convolution fusion | flops 2460352512 | bytes 14166016 | tf_op jit(solution)/shard_map/dot_general | solution.py:50
  181.5 2.3 copy.192
  185.9 2.2 convolution_convert_fusion.6
  193.2 2.3 copy.191
  195.6 3.1 fusion.98
  200.2 1.6 convert_element_type.522
  201.9 1.7 fusion.333
  203.9 3.4 fusion.21
  207.4 3.5 fusion.100
  215.8 28.5 %all_to_all.55 = bf16[16,32,768]{2,1,0:T(8,128)(2,1)S(1)} all-to-all(bf16[16,32,768]{2,1,0:T(8,128)(2,1)S(1)} %broadcast_in_dim.111), channel_id=1, replica_groups=mesh['dp'=16,'section'=2] {'dp'}, dimensions={0} | all-to-all | bytes 1572864 | tf_op jit(solution)/shard_map/all_to_all | solution.py:495
  244.3 9.9 %fusion.337 = (f32[512]{0:T(512)S(1)}, f32[512,7472]{0,1:T(8,128)}) fusion(bf16[512,768]{1,0:T(8,128)(2,1)S(1)} %bitcast.319, bf16[7472,768]{1,0:T(8,128)(2,1)S(1)} %bitcast.292), kind=kOutput, calls=%fused_computation.620 | convolution fusion | flops 5880045056 | bytes 27568128 | tf_op jit(solution)/shard_map/dot_general | solution.py:54
  254.2 10.6 %fusion.69 = bf16[512,768]{1,0:T(8,128)(2,1)} fusion(bf16[7472,768]{1,0:T(8,128)(2,1)S(1)} %bitcast.292, f32[512,7472]{0,1:T(8,128)} %get-tuple-element.170, f32[512]{0:T(512)S(1)} %get-tuple-element.169), kind=kOutput, calls=%fused_computation.131 | convolution fusion | flops 5884264448 | bytes 27568128 | tf_op jit(solution)/shard_map/dot_general | solution.py:50
  264.8 7.4 %fusion.7 = f32[512]{0:T(512)S(1)} fusion(f32[512,7472]{0,1:T(8,128)} %get-tuple-element.170, f32[512]{0:T(512)S(1)} %get-tuple-element.169), kind=kLoop, calls=%fused_computation.15 | loop fusion | flops 7650816 | bytes 15306752 | tf_op jit(solution)/shard_map/reduce_sum | solution.py:489
  276.2 2.2 fusion.110
  278.4 4.7 all-to-all-start.5
  283.8 19.8 %all-to-all-done.5 = bf16[16,32,896]{2,1,0:T(8,128)(2,1)} async-done(((bf16[16,32,896]{2,1,0:T(8,128)(2,1)}), bf16[16,32,896]{2,1,0:T(8,128)(2,1)}, u32[]{:S(2)}, u32[]{:S(2)}) %all-to-all-start.5) | async-done | bytes 917536 | tf_op jit(solution)/shard_map/all_to_all | solution.py:502
  309.1 1.6 fusion.63
  318.7 8.0 %fusion.321 = (f32[32]{0:T(128)}, f32[32]{0:T(128)}, f32[32,768]{1,0:T(8,128)}) fusion(f32[32]{0:T(128)} %copy-done.144, f32[32,768]{1,0:T(8,128)} %copy-done.35, f32[32]{0:T(128)S(1)} %copy-done.127, f32[768]{0:T(1024)S(1)} %copy-done.116, f32[32,768]{1,0:T(8,128)} %convolution_add_fusion.15, bf16[2,768,3072]{2,1,0:T(8,128)(2,1)} %all-gather.11.cloned.1.call-done, ...), kind=kOutput, calls=%fused_computation.606 | convolution fusion | flops 305332160 | bytes 10227584 | tf_op jit(solution)/shard_map/dot_general | solution.py:54
  328.5 2.5 convolution_convert_fusion.5
  332.6 1.8 multiply_reduce_fusion.6
  337.0 3.3 convolution_convert_fusion.3
  340.3 3.5 fusion.92
  344.4 1.7 convert_element_type.564
  346.1 2.0 convolution_add_fusion.13
  349.6 2.9 fusion.64
  353.8 1.8 convert_reduce_fusion.4
  356.4 2.0 convolution_add_fusion
  358.4 17.1 %fusion.320 = (f32[512]{0:T(512)S(1)}, f32[512]{0:T(512)S(1)}, f32[512,768]{0,1:T(8,128)}) fusion(f32[512]{0:T(512)S(1)} %copy-done.101, f32[512,768]{0,1:T(8,128)} %copy-done.20, f32[512]{0:T(512)S(1)} %copy-done.92, f32[768]{0:T(1024)S(1)} %copy-done.88, f32[512,768]{0,1:T(8,128)} %convolution_add_fusion, ...), kind=kOutput, calls=%fused_computation.605 | convolution fusion | flops 4885314560 | bytes 22031360 | tf_op jit(solution)/shard_map/dot_general | solution.py:54
  375.5 3.8 convolution_convert_fusion.2
  380.8 10.2 %multiply_reduce_fusion = (f32[12,512]{1,0:T(8,128)S(1)}, f32[12,512,512]{1,2,0:T(8,128)}) fusion(f32[12,512,512]{1,2,0:T(8,128)} %get-tuple-element.154, f32[12,512]{1,0:T(8,128)S(1)} %copy-done.46, bf16[512,12,64]{0,2,1:T(8,128)(2,1)S(1)} %bitcast.298, bf16[512,12,64]{0,2,1:T(8,128)(2,1)S(1)} %bitcast.297), kind=kOutput, calls=%fused_computation.18 | convolution fusion | flops 412084224 | bytes 26787840 | tf_op jit(solution)/shard_map/qhd,khd->hqk/dot_general | solution.py:174
  393.4 7.1 %multiply_convert_fusion = bf16[12,512,512]{1,2,0:T(8,128)(2,1)S(1)} fusion(f32[12,512,512]{1,2,0:T(8,128)} %get-tuple-element.177, f32[12,512,512]{1,2,0:T(8,128)S(1)} %bitcast.294, f32[12,512]{1,0:T(8,128)S(1)} %get-tuple-element.176, f32[12,512]{1,0:T(8,128)S(1)} %copy-done.46), kind=kLoop, calls=%fused_computation.17 | loop fusion | flops 12582912 | bytes 31506432 | tf_op jit(solution)/shard_map/convert_element_type | solution.py:62
  401.7 2.9 multiply_convert_fusion.7
  404.6 2.0 fusion.74
  407.6 3.6 fusion.66
  417.7 2.2 fusion.319.refs_1_
  422.7 1.9 convolution_add_fusion.9.refs_7_
  426.9 2.6 convolution_add_fusion.11.refs_3_
  430.5 1.9 copy.211.refs_2_
  436.9 2.3 pack_grads.1
  439.3 3.3 collective-permute-done
  442.9 42.0 %all_to_all.56.came_ref = bf16[16,368,128]{2,1,0:T(8,128)(2,1)S(1)} all-to-all(bf16[16,368,128]{2,1,0:T(8,128)(2,1)S(1)} %add_convert_fusion.1), channel_id=1, replica_groups=mesh['dp'=16,'section'=2] {'dp'}, dimensions={0} | all-to-all | bytes 3014656 | tf_op jit(solution)/shard_map/all_to_all | solution.py:554
  485.9 9.7 %all_to_all.57 = f32[32,1,128]{2,1,0:T(1,128)S(1)} all-to-all(f32[32,1,128]{2,1,0:T(1,128)S(1)} %get-tuple-element.72), channel_id=1, replica_groups=mesh['dp'=16,'section'=2] {'dp','section'}, dimensions={0} | all-to-all | bytes 32768 | tf_op jit(solution)/shard_map/all_to_all | solution.py:670
  500.2 1.7 fusion.88
  501.9 1.7 fusion.90
  (522 shorter events, 109.9 us)
Async XLA Ops:
  7.2 490.8 %copy-start = (f32[1,20,48,48]{3,2,1,0:T(8,128)S(1)}, f32[1,20,48,48]{3,2,1,0:T(8,128)}, u32[]{:S(2)}) copy-start(f32[1,20,48,48]{3,2,1,0:T(8,128)} %param.39) | copy-start | bytes 552964
  7.2 83.0 %all-gather.15.cloned.1.call-start = ((), (), s32[]{:S(2)}) async-start(), calls=%async_computation.12 | async-start | bytes 3108864 | tf_op jit(solution)/shard_map/all_gather | solution.py:524
  10.6 98.7 %all-gather.7.cloned.1.call-start = ((), (), s32[]{:S(2)}) async-start(), calls=%async_computation.8 | async-start | bytes 10616832 | tf_op jit(solution)/shard_map/all_gather | solution.py:609
  11.3 132.9 %all-gather.9.cloned.1.call-start = ((), (), s32[]{:S(2)}) async-start(), calls=%async_computation.9 | async-start | bytes 3538944 | tf_op jit(solution)/shard_map/all_gather | solution.py:609
  12.1 6.8 %copy-start.141 = (s32[2,1,32]{2,1,0:T(1,128)S(1)}, s32[2,1,32]{2,1,0:T(1,128)}, u32[]{:S(2)}) copy-start(s32[2,1,32]{2,1,0:T(1,128)} %param.27) | copy-start | bytes 772
  12.1 141.7 %all-gather.11.cloned.1.call-start = ((), (), s32[]{:S(2)}) async-start(), calls=%async_computation.10 | async-start | bytes 14155776 | tf_op jit(solution)/shard_map/all_gather | solution.py:609
  45.7 37.6 %all-to-all-start.3 = ((bf16[16,48,768]{2,1,0:T(8,128)(2,1)}), bf16[16,48,768]{2,1,0:T(8,128)(2,1)S(1)}, u32[]{:S(2)}, u32[]{:S(2)}) async-start(bf16[16,48,768]{2,1,0:T(8,128)(2,1)} %bitcast.9), calls=%async_computation.3 | async-start | bytes 2359296 | tf_op jit(solution)/shard_map/all_to_all | solution.py:456
  49.5 113.7 %all-gather.13.cloned.1.call-start = ((), (), s32[]{:S(2)}) async-start(), calls=%async_computation.11 | async-start | bytes 14155776 | tf_op jit(solution)/shard_map/all_gather | solution.py:609
  50.0 5.7 %copy-start.158 = (s32[2,1,32]{2,1,0:T(1,128)S(1)}, s32[2,1,32]{2,1,0:T(1,128)}, u32[]{:S(2)}) copy-start(s32[2,1,32]{2,1,0:T(1,128)} %param.25) | copy-start | bytes 772
  55.8 107.4 %copy-start.87 = (f32[768]{0:T(1024)}, f32[768]{0:T(1024)S(1)}, u32[]{:S(2)}) copy-start(f32[768]{0:T(1024)S(1)} %get-tuple-element.97) | copy-start | bytes 9220
  55.8 120.7 %copy-start.93 = (f32[768]{0:T(1024)}, f32[768]{0:T(1024)S(1)}, u32[]{:S(2)}) copy-start(f32[768]{0:T(1024)S(1)} %get-tuple-element.95) | copy-start | bytes 9220
  97.9 5.9 %copy-start.134 = (f32[192]{0:T(256)}, f32[192]{0:T(256)S(1)}, u32[]{:S(2)}) copy-start(f32[192]{0:T(256)S(1)} %slice_convert_fusion.14) | copy-start | bytes 2308
  98.5 7.2 %copy-start.136 = (f32[192]{0:T(256)}, f32[192]{0:T(256)S(1)}, u32[]{:S(2)}) copy-start(f32[192]{0:T(256)S(1)} %slice_convert_fusion.13) | copy-start | bytes 2308
  99.1 4.6 copy-start.147
  100.4 6.5 %copy-start.149 = (f32[384]{0:T(512)}, f32[384]{0:T(512)S(1)}, u32[]{:S(2)}) copy-start(f32[384]{0:T(512)S(1)} %get-tuple-element.138) | copy-start | bytes 4612
  103.8 3.9 copy-start.16
  118.2 4.6 copy-start.159
  147.1 16.0 %copy-start.91 = (f32[512]{0:T(512)}, f32[512]{0:T(512)S(1)}, u32[]{:S(2)}) copy-start(f32[512]{0:T(512)S(1)} %broadcast_multiply_fusion.5) | copy-start | bytes 6148
  163.1 11.1 %copy-start.124 = (f32[384]{0:T(512)S(1)}, f32[384]{0:T(512)}, u32[]{:S(2)}) copy-start(f32[384]{0:T(512)} %get-tuple-element.139) | copy-start | bytes 4612
  176.5 3.7 copy-start.106
  181.5 8.3 %copy-start.160 = (pred[512]{0:T(512)(128)(4,1)S(1)}, pred[512]{0:T(512)(128)(4,1)}, u32[]{:S(2)}) copy-start(pred[512]{0:T(512)(128)(4,1)} %iota_compare_fusion.13) | copy-start | bytes 1540
  195.6 8.2 %copy-start.115 = (f32[768]{0:T(1024)S(1)}, f32[768]{0:T(1024)}, u32[]{:S(2)}) copy-start(f32[768]{0:T(1024)} %get-tuple-element.93) | copy-start | bytes 9220
  195.6 8.3 %copy-start.117 = (f32[768]{0:T(1024)S(1)}, f32[768]{0:T(1024)}, u32[]{:S(2)}) copy-start(f32[768]{0:T(1024)} %get-tuple-element.92) | copy-start | bytes 9220
  203.6 3.7 copy-start.35
  203.9 40.4 %slice-start = ((s8[11476992]{0:T(1024)(128)(4,1)}), s8[4194304]{0:T(1024)(128)(4,1)S(1)}, s32[]{:S(2)}) async-start(s8[11476992]{0:T(1024)(128)(4,1)} %bitcast.291), calls=%async_computation.13 | async-start | bytes 8388608
  207.4 3.9 copy-start.138
  207.4 36.9 %slice-start.1 = ((s8[11476992]{0:T(1024)(128)(4,1)}), s8[4194304]{0:T(1024)(128)(4,1)S(1)}, s32[]{:S(2)}) async-start(s8[11476992]{0:T(1024)(128)(4,1)} %bitcast.291), calls=%async_computation.14 | async-start | bytes 8388608
  207.4 36.9 %slice-start.2 = ((s8[11476992]{0:T(1024)(128)(4,1)}), s8[3088384]{0:T(1024)(128)(4,1)S(1)}, s32[]{:S(2)}) async-start(s8[11476992]{0:T(1024)(128)(4,1)} %bitcast.291), calls=%async_computation.15 | async-start | bytes 6176768
  278.4 25.2 %all-to-all-start.5 = ((bf16[16,32,896]{2,1,0:T(8,128)(2,1)}), bf16[16,32,896]{2,1,0:T(8,128)(2,1)}, u32[]{:S(2)}, u32[]{:S(2)}) async-start(bf16[16,32,896]{2,1,0:T(8,128)(2,1)} %bitcast.306), calls=%async_computation.5 | async-start | bytes 1835008 | tf_op jit(solution)/shard_map/all_to_all | solution.py:502
  307.6 3.8 copy-start.31
  307.6 3.8 copy-start.52
  307.6 3.8 copy-start.105
  307.6 3.8 copy-start.121
  307.6 3.8 copy-start.132
  307.6 5.0 copy-start.82
  307.6 6.6 %copy-start.85 = (f32[32,192]{1,0:T(8,128)S(1)}, f32[32,192]{1,0:T(8,128)}, u32[]{:S(2)}) copy-start(f32[32,192]{1,0:T(8,128)} %copy-done.84) | copy-start | bytes 73732
  309.1 6.1 %copy-start.34 = (f32[32,768]{1,0:T(8,128)S(1)}, f32[32,768]{1,0:T(8,128)}, u32[]{:S(2)}) copy-start(f32[32,768]{1,0:T(8,128)} %copy-done.33) | copy-start | bytes 294916
  309.1 6.1 %copy-start.96 = (f32[768]{0:T(1024)S(1)}, f32[768]{0:T(1024)}, u32[]{:S(2)}) copy-start(f32[768]{0:T(1024)} %get-tuple-element.88) | copy-start | bytes 9220
  309.1 6.1 %copy-start.119 = (f32[32]{0:T(128)S(1)}, f32[32]{0:T(128)}, u32[]{:S(2)}) copy-start(f32[32]{0:T(128)} %copy-done.118) | copy-start | bytes 388
  309.1 6.1 %copy-start.130 = (f32[32]{0:T(128)S(1)}, f32[32]{0:T(128)}, u32[]{:S(2)}) copy-start(f32[32]{0:T(128)} %copy-done.129) | copy-start | bytes 388
  310.8 5.4 %copy-start.79 = (f32[32,384]{1,0:T(8,128)S(1)}, f32[32,384]{1,0:T(8,128)}, u32[]{:S(2)}) copy-start(f32[32,384]{1,0:T(8,128)} %copy-done.78) | copy-start | bytes 147460
  314.3 4.4 copy-start.116
  314.3 4.4 copy-start.127
  327.3 7.1 %copy-start.161 = (f32[32]{0:T(128)}, f32[32]{0:T(128)S(1)}, u32[]{:S(2)}) copy-start(f32[32]{0:T(128)S(1)} %broadcast_multiply_fusion.7) | copy-start | bytes 388
  340.2 5.8 %copy-start.128 = (f32[32]{0:T(128)S(1)}, f32[32]{0:T(128)}, u32[]{:S(2)}) copy-start(f32[32]{0:T(128)} %copy-done.126) | copy-start | bytes 388
  344.4 5.1 copy-start.94
  344.4 5.1 copy-start.103
  344.4 5.1 copy-start.107
  358.4 17.1 %copy-start.21 = (f32[512,768]{0,1:T(8,128)S(1)}, f32[512,768]{0,1:T(8,128)}, u32[]{:S(2)}) copy-start(f32[512,768]{0,1:T(8,128)} %copy-done.20) | copy-start | bytes 4718596
  375.5 3.8 copy-start.152
  375.5 5.3 %copy-start.46 = (f32[12,512]{1,0:T(8,128)S(1)}, f32[12,512]{1,0:T(8,128)}, u32[]{:S(2)}) copy-start(f32[12,512]{1,0:T(8,128)} %copy-done.45) | copy-start | bytes 73732
  380.8 10.3 %slice-start.3 = ((s8[12582912]{0:T(1024)(128)(4,1)}), s8[4194304]{0:T(1024)(128)(4,1)S(1)}, s32[]{:S(2)}) async-start(s8[12582912]{0:T(1024)(128)(4,1)} %bitcast.293), calls=%async_computation.16 | async-start | bytes 8388608
  380.8 11.4 %slice-start.4 = ((s8[12582912]{0:T(1024)(128)(4,1)}), s8[4194304]{0:T(1024)(128)(4,1)S(1)}, s32[]{:S(2)}) async-start(s8[12582912]{0:T(1024)(128)(4,1)} %bitcast.293), calls=%async_computation.17 | async-start | bytes 8388608
  380.8 12.6 %slice-start.5 = ((s8[12582912]{0:T(1024)(128)(4,1)}), s8[4194304]{0:T(1024)(128)(4,1)S(1)}, s32[]{:S(2)}) async-start(s8[12582912]{0:T(1024)(128)(4,1)} %bitcast.293), calls=%async_computation.18 | async-start | bytes 8388608
  393.4 7.1 %copy-start.15 = (bf16[512,768]{0,1:T(8,128)(2,1)S(1)}, bf16[512,768]{0,1:T(8,128)(2,1)}, u32[]{:S(2)}) copy-start(bf16[512,768]{0,1:T(8,128)(2,1)} %copy.186) | copy-start | bytes 2359300
  401.7 5.0 slice-start.6
  411.1 9.4 %copy-start.38 = (f32[512,768]{0,1:T(8,128)}, f32[512,768]{0,1:T(8,128)S(1)}, u32[]{:S(2)}) copy-start(f32[512,768]{0,1:T(8,128)S(1)} %fusion.66) | copy-start | bytes 4718596
  411.8 8.7 %copy-start.48 = (bf16[512,192]{0,1:T(8,128)(2,1)}, bf16[512,192]{0,1:T(8,128)(2,1)S(1)}, u32[]{:S(2)}) copy-start(bf16[512,192]{0,1:T(8,128)(2,1)S(1)} %get-tuple-element.183) | copy-start | bytes 589828
  439.2 3.4 collective-permute-start
  442.9 54.1 %copy-start.27 = (f32[1,20,48,48]{3,2,1,0:T(8,128)S(1)}, f32[1,20,48,48]{3,2,1,0:T(8,128)}, u32[]{:S(2)}) copy-start(f32[1,20,48,48]{3,2,1,0:T(8,128)} %param.36) | copy-start | bytes 552964
  499.4 4.2 copy-start.29
  499.4 4.2 copy-start.155
  499.4 4.2 copy-start.163
  499.4 4.2 copy-start.164
  (117 other events, 231.7 us)
Sparse Core Ops, SparseCore 0:
  11.5 68.8 all-gather.14
  81.9 18.5 all-gather.6
  102.0 12.1 all-gather.8
  115.6 23.0 all-gather.10
  140.1 23.0 all-gather.12
